TPU v7x, 32 devices: a whole 2x2x4 slice. The times are simulated.
32 devices in a mesh: row: 8 (over z, core), col: 4 (over y, x).
Axes of the slice: x: 2, y: 2, z: 4, core: 2. Of those that a mesh axis runs over, the one named last changes fastest.
Arguments:
- multipliers: float32 [32, 2, 16, 256], P(('row', 'col')), may hold values from -6 to 6
- residual: float32 [32, 2, 16, 256], P(('row', 'col')), may hold values from -18 to 18
- direction: float32 [32, 2, 16, 256], P(('row', 'col')), may hold values from -6 to 6
- energy_prev: float32 [16], replicated, may hold values from 32768 to 131072
- hypersingular: bfloat16 [32, 1152, 1152], P(('row', 'col')), may hold values from -1 to 4, as said below
- double_layer: bfloat16 [32, 1152, 1152], P(('row', 'col')), may hold values from -0.1875 to 0.1875
- single_inverse: bfloat16 [32, 1152, 1152], P(('row', 'col')), may hold values from -1 to 4, as said below
- neumann_inverse: bfloat16 [32, 1152, 1152], P(('row', 'col')), may hold values from -1 to 4, as said below
- rigid_modes: float32 [32, 6, 1152], P(('row', 'col')), may hold values from -0.75 to 0.75
- coarse_inverse: float32 [192, 192], P(('row', 'col')), may hold values from -0.875 to 0.875
- face_index: int32 [32, 4, 256], P(('row', 'col')), may hold values from 0 to 1151, as said below
Outputs:
- multipliers_next: float32 [32, 2, 16, 256], P(('row', 'col'))
- residual_next: float32 [32, 2, 16, 256], P(('row', 'col'))
- direction_next: float32 [32, 2, 16, 256], P(('row', 'col'))
Inputs may be any that keep to these rules, and one draw needn't show every extreme that they name: For each patch the 1024 entries of face_index are distinct. `hypersingular`: each patch's matrix is symmetric positive definite. `single_inverse`: each patch's matrix is symmetric positive definite. `neumann_inverse`: each patch's matrix is symmetric positive definite.
All inputs are finite; a program needn't handle non-finite values.
Results may differ from a plain program's by a relative error of at most 0.0015.
Values sent between devices are 32-bit elements; how exact they have to be, the bound alone decides.
A program may use at most 64 MiB of HBM per device.

v0:
```python
import jax
import jax.numpy as jnp
from jax import lax
from jax.sharding import PartitionSpec as P

NB = 1152


highest = lax.Precision.HIGHEST
contract_last = (((1,), (1,)), ((), ()))
contract_first = (((0,), (0,)), ((), ()))


def shifted(block, axis, distance):
    devices = range(lax.axis_size(axis))
    route = [((i - distance) % len(devices), i) for i in devices]
    return lax.ppermute(block, axis, route)


def spread_faces(values, face_where):
    from_left = shifted(values[0], "col", 1)
    from_below = shifted(values[1], "row", 1)
    pieces = jnp.concatenate([values[0], values[1], -from_left, -from_below], axis=1)
    return jnp.zeros((values.shape[1], NB), jnp.float32).at[:, face_where].set(pieces)


def jump_faces(vectors, face_where):
    face_width = face_where.shape[0] // 4
    picked = jnp.take(vectors, face_where, axis=1)
    from_right = shifted(picked[:, 2 * face_width : 3 * face_width], "col", -1)
    from_above = shifted(picked[:, 3 * face_width :], "row", -1)
    return jnp.stack(
        [picked[:, :face_width] - from_right, picked[:, face_width : 2 * face_width] - from_above]
    )


def project(values, face_where, rigid_local, coarse_rows):
    spread = spread_faces(values, face_where)
    partial_value = lax.dot_general(rigid_local, spread, contract_last, precision=highest)
    coarse_coef = jnp.dot(
        coarse_rows,
        lax.all_gather(partial_value, ("row", "col"), axis=0, tiled=True),
        precision=highest,
    )
    modes_back = lax.dot_general(coarse_coef, rigid_local, contract_first, precision=highest)
    correction = jump_faces(modes_back, face_where)
    return values - correction


def on_device(
    multipliers,
    residual,
    direction,
    energy_prev,
    hypersingular,
    double_layer,
    single_inverse,
    neumann_inverse,
    rigid_modes,
    coarse_inverse,
    face_index,
):
    face_where = face_index[0].reshape(-1)
    rigid_local = rigid_modes[0]
    hyper_local = hypersingular[0]
    double_local = double_layer[0]
    single_local = single_inverse[0]
    neumann_local = neumann_inverse[0]
    multipliers_now = multipliers[0]
    residual_now = residual[0]
    direction_now = direction[0]
    cases = residual_now.shape[1]
    projected = project(residual_now, face_where, rigid_local, coarse_inverse)
    rounded = spread_faces(projected, face_where).astype(jnp.bfloat16)
    lifted = (
        0.5 * rounded.astype(jnp.float32)
        + jnp.dot(rounded, double_local, preferred_element_type=jnp.float32)
    ).astype(jnp.bfloat16)
    weighed = jnp.dot(lifted, single_local, preferred_element_type=jnp.float32).astype(jnp.bfloat16)
    applied = (
        jnp.dot(rounded, hyper_local, preferred_element_type=jnp.float32)
        + 0.5 * weighed.astype(jnp.float32)
        + lax.dot_general(weighed, double_local, contract_last, preferred_element_type=jnp.float32)
    )
    energy_local = jnp.sum(rounded.astype(jnp.float32) * applied, axis=1)
    searched = project(jump_faces(applied, face_where), face_where, rigid_local, coarse_inverse)
    paired = spread_faces(jnp.concatenate([searched, direction_now], axis=1), face_where).astype(
        jnp.bfloat16
    )
    paired_applied = jnp.dot(paired, neumann_local, preferred_element_type=jnp.float32)
    paired_new = paired[:cases].astype(jnp.float32)
    paired_old = paired[cases:].astype(jnp.float32)
    applied_new = paired_applied[:cases]
    applied_old = paired_applied[cases:]
    self_local = jnp.sum(paired_new * applied_new, axis=1)
    cross_local = jnp.sum(paired_new * applied_old + paired_old * applied_new, axis=1)
    old_local = jnp.sum(paired_old * applied_old, axis=1)
    energy, self_term, cross_term, old_term = lax.psum(
        (energy_local, self_local, cross_local, old_local), ("row", "col")
    )
    step_ratio = energy / energy_prev
    curvature = self_term + step_ratio * (cross_term + step_ratio * old_term)
    applied_dir = applied_new + step_ratio[:, None] * applied_old
    step_size = energy / curvature
    direction_now = searched + step_ratio[None, :, None] * direction_now
    multipliers_now = multipliers_now + step_size[None, :, None] * direction_now
    corrected = project(
        jump_faces(applied_dir, face_where), face_where, rigid_local, coarse_inverse
    )
    residual_now = residual_now - step_size[None, :, None] * corrected
    return (multipliers_now[None], residual_now[None], direction_now[None])


def solution(mesh):
    return jax.shard_map(
        on_device,
        mesh=mesh,
        in_specs=(
            P(("row", "col"), None, None, None),
            P(("row", "col"), None, None, None),
            P(("row", "col"), None, None, None),
            P(),
            P(("row", "col"), None, None),
            P(("row", "col"), None, None),
            P(("row", "col"), None, None),
            P(("row", "col"), None, None),
            P(("row", "col"), None, None),
            P(("row", "col"), None),
            P(("row", "col"), None, None),
        ),
        out_specs=(
            P(("row", "col"), None, None, None),
            P(("row", "col"), None, None, None),
            P(("row", "col"), None, None, None),
        ),
        check_vma=False,
    )
```

profile of v0, /device:TPU:0, one launch (start us, length us, event | category | flops | bytes accessed | tf_op | source)
XLA Modules:
  0.0 372.2 jit_solution(268122889715842178)
XLA Ops:
  1.5 2.9 collective-permute-start
  7.1 2.3 collective-permute-done.1
  10.5 3.6 scatter_custom_fusion
  15.3 65.5 %all-gather = f32[32,6,16]{2,1,0:T(8,128)S(1)} all-gather(f32[1,6,16]{2,1,0:T(8,128)S(1)} %convolution_bitcast_fusion.2), channel_id=1, replica_groups=mesh['row'=8,'col'=4] {'row','col'}, dimensions={0}, use_global_device_ids=true | all-gather | bytes 12672 | tf_op jit(solution)/shard_map/all_gather | solution.py:42
  83.6 4.0 %gather_fusion = f32[1024,16]{1,0:T(8,128)} fusion(f32[16,1152]{0,1:T(8,128)S(1)} %fusion.56, s32[1024]{0:T(1024)S(1)} %fusion.72), kind=kCustom, calls=%fused_computation.clone | custom fusion | bytes 135168 | tf_op jit(solution)/shard_map/jit(_take)/gather | solution.py:29
  88.9 5.0 %collective-permute-done.2 = f32[16,256]{0,1:T(8,128)S(1)} collective-permute-done((f32[16,256]{0,1:T(8,128)S(1)}, f32[16,256]{0,1:T(8,128)S(1)}, u32[]{:S(2)}, u32[]{:S(2)}) %collective-permute-start.2) | collective-permute-done | bytes 16416 | tf_op jit(solution)/shard_map/ppermute | solution.py:17
  94.6 2.8 collective-permute-done.3
  99.5 2.7 collective-permute-done.4
  102.2 2.3 collective-permute-done.5
  105.5 3.6 scatter_custom_fusion.1
  109.2 2.6 fusion.22
  114.9 4.0 %gather_fusion.1 = f32[1024,16]{1,0:T(8,128)} fusion(f32[16,1152]{0,1:T(8,128)S(1)} %copy.88, s32[1024]{0:T(1024)S(1)} %fusion.72), kind=kCustom, calls=%fused_computation.1.clone | custom fusion | bytes 135168 | tf_op jit(solution)/shard_map/jit(_take)/gather | solution.py:29
  121.2 2.8 collective-permute-done.6
  125.4 3.2 collective-permute-done.8
  131.4 3.6 scatter_custom_fusion.2
  135.5 65.2 %all-gather.1 = f32[32,6,16]{2,1,0:T(8,128)S(1)} all-gather(f32[1,6,16]{2,1,0:T(8,128)S(1)} %convolution_bitcast_fusion.1), channel_id=1, replica_groups=mesh['row'=8,'col'=4] {'row','col'}, dimensions={0}, use_global_device_ids=true | all-gather | bytes 12672 | tf_op jit(solution)/shard_map/all_gather | solution.py:42
  202.0 4.0 %gather_fusion.2 = f32[1024,16]{1,0:T(8,128)} fusion(f32[16,1152]{0,1:T(8,128)S(1)} %fusion.53, s32[1024]{0:T(1024)S(1)} %fusion.72), kind=kCustom, calls=%fused_computation.2.clone | custom fusion | bytes 135168 | tf_op jit(solution)/shard_map/jit(_take)/gather | solution.py:29
  207.4 4.9 %collective-permute-done.10 = f32[16,256]{0,1:T(8,128)S(1)} collective-permute-done((f32[16,256]{0,1:T(8,128)S(1)}, f32[16,256]{0,1:T(8,128)S(1)}, u32[]{:S(2)}, u32[]{:S(2)}) %collective-permute-start.10) | collective-permute-done | bytes 16416 | tf_op jit(solution)/shard_map/ppermute | solution.py:17
  213.3 2.4 collective-permute-start.12
  215.6 2.7 collective-permute-done.12
  218.3 2.4 collective-permute-done.13
  221.8 3.6 scatter_custom_fusion.3
  225.6 2.3 fusion
  228.1 37.1 %all-reduce = (f32[16]{0:T(128)S(1)}, f32[16]{0:T(128)S(1)}, f32[16]{0:T(128)S(1)}, f32[16]{0:T(128)S(1)}) all-reduce(f32[16]{0:T(128)} %get-tuple-element.44, f32[16]{0:T(128)S(1)} %get-tuple-element.12, f32[16]{0:T(128)S(1)} %get-tuple-element.11, f32[16]{0:T(128)S(1)} %get-tuple-element.10), channel_id=1, replica_groups=mesh['row'=8,'col'=4] {'row','col'}, use_global_device_ids=true, to_apply=%region_3.5 | all-reduce | flops 64 | bytes 512 | tf_op jit(solution)/shard_map/psum | solution.py:98
  266.7 4.0 %gather_fusion.3 = f32[1024,16]{1,0:T(8,128)} fusion(f32[16,1152]{0,1:T(8,128)S(1)} %copy.98, s32[1024]{0:T(1024)S(1)} %fusion.72), kind=kCustom, calls=%fused_computation.3.clone | custom fusion | bytes 135168 | tf_op jit(solution)/shard_map/jit(_take)/gather | solution.py:29
  273.8 2.2 collective-permute-done.14
  276.0 3.0 collective-permute-start.16
  280.7 3.3 collective-permute-done.17
  285.0 3.7 scatter_custom_fusion.4
  289.1 65.4 %all-gather.2 = f32[32,6,16]{2,1,0:T(8,128)S(1)} all-gather(f32[1,6,16]{2,1,0:T(8,128)S(1)} %convolution_bitcast_fusion), channel_id=1, replica_groups=mesh['row'=8,'col'=4] {'row','col'}, dimensions={0}, use_global_device_ids=true | all-gather | bytes 12672 | tf_op jit(solution)/shard_map/all_gather | solution.py:42
  355.9 4.0 %gather_fusion.4 = f32[1024,16]{1,0:T(8,128)} fusion(f32[16,1152]{0,1:T(8,128)S(1)} %fusion.50, s32[1024]{0:T(1024)S(1)} %fusion.72), kind=kCustom, calls=%fused_computation.4.clone | custom fusion | bytes 135168 | tf_op jit(solution)/shard_map/jit(_take)/gather | solution.py:29
  361.2 5.0 %collective-permute-done.18 = f32[16,256]{0,1:T(8,128)S(1)} collective-permute-done((f32[16,256]{0,1:T(8,128)S(1)}, f32[16,256]{0,1:T(8,128)S(1)}, u32[]{:S(2)}, u32[]{:S(2)}) %collective-permute-start.18) | collective-permute-done | bytes 16416 | tf_op jit(solution)/shard_map/ppermute | solution.py:17
  (137 shorter events, 45.2 us)
Async XLA Ops:
  0.6 108.6 %copy-start = (bf16[1,1152,1152]{2,1,0:T(8,128)(2,1)S(1)}, bf16[1,1152,1152]{2,1,0:T(8,128)(2,1)}, u32[]{:S(2)}) copy-start(bf16[1,1152,1152]{2,1,0:T(8,128)(2,1)} %param.18) | copy-start | bytes 7962628
  1.5 5.6 %collective-permute-start = (f32[16,256]{1,0:T(8,128)S(1)}, f32[16,256]{1,0:T(8,128)S(1)}, u32[]{:S(2)}, u32[]{:S(2)}) collective-permute-start(f32[16,256]{1,0:T(8,128)S(1)} %get-tuple-element.41), channel_id=1, source_target_pairs={{3,0},{0,1},{1,2},{2,3},{7,4},{4,5},{5,6},{6,7},{11,8},{8,9},{9,10... | collective-permute-start | bytes 49160 | tf_op jit(solution)/shard_map/ppermute | solution.py:17
  4.5 5.0 %collective-permute-start.1 = (f32[16,256]{1,0:T(8,128)S(1)}, f32[16,256]{1,0:T(8,128)S(1)}, u32[]{:S(2)}, u32[]{:S(2)}) collective-permute-start(f32[16,256]{1,0:T(8,128)S(1)} %get-tuple-element.42), channel_id=1, source_target_pairs={{28,0},{0,4},{4,8},{8,12},{12,16},{16,20},{20,24},{24,28},{29,1},{... | collective-permute-start | bytes 49160 | tf_op jit(solution)/shard_map/ppermute | solution.py:17
  5.2 100.3 %copy-start.15 = (s32[1024,1]{0,1:T(1,128)}, s32[1024,1]{0,1:T(1,128)S(1)}, u32[]{:S(2)}) copy-start(s32[1024,1]{0,1:T(1,128)S(1)} %compare_select_fusion) | copy-start | bytes 12292
  5.9 200.1 %copy-start.11 = (pred[1024]{0:T(1024)(128)(4,1)}, pred[1024]{0:T(1024)(128)(4,1)S(1)}, u32[]{:S(2)}) copy-start(pred[1024]{0:T(1024)(128)(4,1)S(1)} %compare_and_fusion) | copy-start | bytes 3076
  10.5 87.0 %copy-start.4 = (f32[1,2,16,256]{3,2,1,0:T(8,128)S(1)}, f32[1,2,16,256]{3,2,1,0:T(8,128)}, u32[]{:S(2)}) copy-start(f32[1,2,16,256]{3,2,1,0:T(8,128)} %param.14) | copy-start | bytes 98308
  88.8 5.0 %collective-permute-start.2 = (f32[16,256]{0,1:T(8,128)S(1)}, f32[16,256]{0,1:T(8,128)S(1)}, u32[]{:S(2)}, u32[]{:S(2)}) collective-permute-start(f32[16,256]{0,1:T(8,128)S(1)} %slice.139), channel_id=1, source_target_pairs={{1,0},{2,1},{3,2},{0,3},{5,4},{6,5},{7,6},{4,7},{9,8},{10,9},{11,1... | collective-permute-start | bytes 49160 | tf_op jit(solution)/shard_map/ppermute | solution.py:17
  94.5 2.8 collective-permute-start.3
  97.5 4.7 %collective-permute-start.4 = (f32[16,256]{1,0:T(8,128)S(1)}, f32[16,256]{1,0:T(8,128)S(1)}, u32[]{:S(2)}, u32[]{:S(2)}) collective-permute-start(f32[16,256]{1,0:T(8,128)S(1)} %get-tuple-element.39), channel_id=1, source_target_pairs={{3,0},{0,1},{1,2},{2,3},{7,4},{4,5},{5,6},{6,7},{11,8},{8,9},{9,10... | collective-permute-start | bytes 49160 | tf_op jit(solution)/shard_map/ppermute | solution.py:17
  99.5 5.0 %collective-permute-start.5 = (f32[16,256]{1,0:T(8,128)S(1)}, f32[16,256]{1,0:T(8,128)S(1)}, u32[]{:S(2)}, u32[]{:S(2)}) collective-permute-start(f32[16,256]{1,0:T(8,128)S(1)} %get-tuple-element.40), channel_id=1, source_target_pairs={{28,0},{0,4},{4,8},{8,12},{12,16},{16,20},{20,24},{24,28},{29,1},{... | collective-permute-start | bytes 49160 | tf_op jit(solution)/shard_map/ppermute | solution.py:17
  113.6 21.5 %copy-start.2 = (f32[1,6,1152]{2,0,1:T(1,128)S(1)}, f32[1,6,1152]{2,0,1:T(1,128)}, u32[]{:S(2)}) copy-start(f32[1,6,1152]{2,0,1:T(1,128)} %param.21) | copy-start | bytes 82948
  114.7 86.0 %copy-start.10 = (f32[6,192]{1,0:T(8,128)S(1)}, f32[6,192]{1,0:T(8,128)}, u32[]{:S(2)}) copy-start(f32[6,192]{1,0:T(8,128)} %param.22) | copy-start | bytes 13828
  120.2 3.8 %collective-permute-start.6 = (f32[16,256]{1,0:T(8,128)S(1)}, f32[16,256]{1,0:T(8,128)S(1)}, u32[]{:S(2)}, u32[]{:S(2)}) collective-permute-start(f32[16,256]{1,0:T(8,128)S(1)} %slice.145), channel_id=1, source_target_pairs={{1,0},{2,1},{3,2},{0,3},{5,4},{6,5},{7,6},{4,7},{9,8},{10,9},{11,1... | collective-permute-start | bytes 49160 | tf_op jit(solution)/shard_map/ppermute | solution.py:17
  124.0 1.4 collective-permute-start.7
  124.0 4.7 %collective-permute-start.8 = (f32[16,256]{1,0:T(8,128)S(1)}, f32[16,256]{1,0:T(8,128)S(1)}, u32[]{:S(2)}, u32[]{:S(2)}) collective-permute-start(f32[16,256]{1,0:T(8,128)S(1)} %get-tuple-element.37), channel_id=1, source_target_pairs={{3,0},{0,1},{1,2},{2,3},{7,4},{4,5},{5,6},{6,7},{11,8},{8,9},{9,10... | collective-permute-start | bytes 49160 | tf_op jit(solution)/shard_map/ppermute | solution.py:17
  125.4 87.8 %copy-start.5 = (f32[16,256]{1,0:T(8,128)}, f32[16,256]{1,0:T(8,128)S(1)}, u32[]{:S(2)}) copy-start(f32[16,256]{1,0:T(8,128)S(1)} %slice_subtract_fusion.8) | copy-start | bytes 49156
  125.4 5.0 %collective-permute-start.9 = (f32[16,256]{1,0:T(8,128)S(1)}, f32[16,256]{1,0:T(8,128)S(1)}, u32[]{:S(2)}, u32[]{:S(2)}) collective-permute-start(f32[16,256]{1,0:T(8,128)S(1)} %slice_subtract_fusion.8), channel_id=1, source_target_pairs={{28,0},{0,4},{4,8},{8,12},{12,16},{16,20},{20,24},{24,28},{29,1},{... | collective-permute-start | bytes 49160 | tf_op jit(solution)/shard_map/ppermute | solution.py:17
  135.0 78.2 %copy-start.9 = (f32[1,2,16,256]{3,2,1,0:T(8,128)S(1)}, f32[1,2,16,256]{3,2,1,0:T(8,128)}, u32[]{:S(2)}) copy-start(f32[1,2,16,256]{3,2,1,0:T(8,128)} %param.15) | copy-start | bytes 98308
  207.3 5.0 %collective-permute-start.10 = (f32[16,256]{0,1:T(8,128)S(1)}, f32[16,256]{0,1:T(8,128)S(1)}, u32[]{:S(2)}, u32[]{:S(2)}) collective-permute-start(f32[16,256]{0,1:T(8,128)S(1)} %get-tuple-element.29), channel_id=1, source_target_pairs={{1,0},{2,1},{3,2},{0,3},{5,4},{6,5},{7,6},{4,7},{9,8},{10,9},{11,1... | collective-permute-start | bytes 49160 | tf_op jit(solution)/shard_map/ppermute | solution.py:17
  207.4 5.0 %collective-permute-start.11 = (f32[16,256]{0,1:T(8,128)S(1)}, f32[16,256]{0,1:T(8,128)S(1)}, u32[]{:S(2)}, u32[]{:S(2)}) collective-permute-start(f32[16,256]{0,1:T(8,128)S(1)} %get-tuple-element.30), channel_id=1, source_target_pairs={{4,0},{8,4},{12,8},{16,12},{20,16},{24,20},{28,24},{0,28},{5,1},{9... | collective-permute-start | bytes 49160 | tf_op jit(solution)/shard_map/ppermute | solution.py:17
  213.3 5.0 %collective-permute-start.12 = (f32[32,256]{1,0:T(8,128)S(1)}, f32[32,256]{1,0:T(8,128)S(1)}, u32[]{:S(2)}, u32[]{:S(2)}) collective-permute-start(f32[32,256]{1,0:T(8,128)S(1)} %get-tuple-element.35), channel_id=1, source_target_pairs={{3,0},{0,1},{1,2},{2,3},{7,4},{4,5},{5,6},{6,7},{11,8},{8,9},{9,10... | collective-permute-start | bytes 98312 | tf_op jit(solution)/shard_map/ppermute | solution.py:17
  215.6 5.1 %collective-permute-start.13 = (f32[32,256]{1,0:T(8,128)S(1)}, f32[32,256]{1,0:T(8,128)S(1)}, u32[]{:S(2)}, u32[]{:S(2)}) collective-permute-start(f32[32,256]{1,0:T(8,128)S(1)} %get-tuple-element.36), channel_id=1, source_target_pairs={{28,0},{0,4},{4,8},{8,12},{12,16},{16,20},{20,24},{24,28},{29,1},{... | collective-permute-start | bytes 98312 | tf_op jit(solution)/shard_map/ppermute | solution.py:17
  225.6 46.3 %copy-start.12 = (pred[1024]{0:T(1024)(128)(4,1)S(1)}, pred[1024]{0:T(1024)(128)(4,1)}, u32[]{:S(2)}) copy-start(pred[1024]{0:T(1024)(128)(4,1)} %copy-done.11) | copy-start | bytes 3076
  266.4 18.7 %copy-start.13 = (f32[16]{0:T(128)}, f32[16]{0:T(128)S(1)}, u32[]{:S(2)}) copy-start(f32[16]{0:T(128)S(1)} %get-tuple-element.20) | copy-start | bytes 196
  271.9 4.0 %collective-permute-start.14 = (f32[16,256]{1,0:T(8,128)S(1)}, f32[16,256]{1,0:T(8,128)S(1)}, u32[]{:S(2)}, u32[]{:S(2)}) collective-permute-start(f32[16,256]{1,0:T(8,128)S(1)} %slice.159), channel_id=1, source_target_pairs={{1,0},{2,1},{3,2},{0,3},{5,4},{6,5},{7,6},{4,7},{9,8},{10,9},{11,1... | collective-permute-start | bytes 49160 | tf_op jit(solution)/shard_map/ppermute | solution.py:17
  276.0 3.0 collective-permute-start.15
  276.0 4.7 %collective-permute-start.16 = (f32[16,256]{1,0:T(8,128)S(1)}, f32[16,256]{1,0:T(8,128)S(1)}, u32[]{:S(2)}, u32[]{:S(2)}) collective-permute-start(f32[16,256]{1,0:T(8,128)S(1)} %get-tuple-element.33), channel_id=1, source_target_pairs={{3,0},{0,1},{1,2},{2,3},{7,4},{4,5},{5,6},{6,7},{11,8},{8,9},{9,10... | collective-permute-start | bytes 49160 | tf_op jit(solution)/shard_map/ppermute | solution.py:17
  279.0 5.0 %collective-permute-start.17 = (f32[16,256]{1,0:T(8,128)S(1)}, f32[16,256]{1,0:T(8,128)S(1)}, u32[]{:S(2)}, u32[]{:S(2)}) collective-permute-start(f32[16,256]{1,0:T(8,128)S(1)} %slice_subtract_fusion.6), channel_id=1, source_target_pairs={{28,0},{0,4},{4,8},{8,12},{12,16},{16,20},{20,24},{24,28},{29,1},{... | collective-permute-start | bytes 49160 | tf_op jit(solution)/shard_map/ppermute | solution.py:17
  285.0 82.8 %copy-start.3 = (f32[1,1,16,256]{2,3,1,0:T(8,128)S(1)}, f32[1,1,16,256]{2,3,1,0:T(8,128)}, u32[]{:S(2)}) copy-start(f32[1,1,16,256]{2,3,1,0:T(8,128)} %get-tuple-element.28) | copy-start | bytes 49156
  288.7 81.9 %copy-start.6 = (f32[16,256]{1,0:T(8,128)S(1)}, f32[16,256]{1,0:T(8,128)}, u32[]{:S(2)}) copy-start(f32[16,256]{1,0:T(8,128)} %copy-done.5) | copy-start | bytes 49156
  361.1 5.0 %collective-permute-start.18 = (f32[16,256]{0,1:T(8,128)S(1)}, f32[16,256]{0,1:T(8,128)S(1)}, u32[]{:S(2)}, u32[]{:S(2)}) collective-permute-start(f32[16,256]{0,1:T(8,128)S(1)} %slice.163), channel_id=1, source_target_pairs={{1,0},{2,1},{3,2},{0,3},{5,4},{6,5},{7,6},{4,7},{9,8},{10,9},{11,1... | collective-permute-start | bytes 49160 | tf_op jit(solution)/shard_map/ppermute | solution.py:17
  366.8 2.8 collective-permute-start.19
  (4 other events, 30.8 us)
where the time goes:
time: 373 us; the launch traced here: 372 us
  blocking collectives  233 us (62%)
  local copies, waits for them, and re-layouts  51.7 us (14%)
  waiting for transfers between devices  45.9 us (12%)
  starting transfers between devices  16.2 us (4%)
  matrix products  14.2 us (4%)
  other arithmetic  9.84 us (3%)
    all_gather x3, blocking collectives, project(): lax.all_gather(partial_value, ('row', 'col'), axis=0, tiled=True)  196 us
    ppermute x20, waiting for transfers between devices, shifted(): return lax.ppermute(block, axis, route)  45.9 us
    psum x1, blocking collectives, on_device(): lax.psum((energy_local, self_local, cross_local, old_local), ('row', 'col'))  37.1 us
    gather x7, local copies, waits for them, and re-layouts, jump_faces(): picked = jnp.take(vectors, face_where, axis=1)  22.4 us
    scatter x7, local copies, waits for them, and re-layouts, spread_faces(): jnp.zeros((values.shape[1], NB), jnp.float32).at[:, face_where].set(pieces)  18.4 us
    ppermute x20, starting transfers between devices, shifted(): return lax.ppermute(block, axis, route)  16.2 us
  transfers between devices with their start and end apart: 20, of which 17 were waited for; matrix products, arithmetic and copies ran while one was open for 1% of the time, Pallas kernels for 0%

commit v1 on v0

v1 whole, which is shorter than its diff:
```python
import functools

import jax
import jax.numpy as jnp
from jax import lax
from jax.experimental import pallas as pl
from jax.experimental.pallas import tpu as pltpu
from jax.sharding import PartitionSpec as P

MESH = pl.DeviceIdType.MESH
NN = (((1,), (0,)), ((), ()))
NT = (((1,), (1,)), ((), ()))
f32 = jnp.float32
bf16 = jnp.bfloat16
GROUPS = 8
SLOTS = 8


def mul(a, b, dims=NN):
    return lax.dot_general(a, b, dims, preferred_element_type=f32)


def split2(x):
    high = x.astype(bf16)
    return high, (x - high.astype(f32)).astype(bf16)


def mul_exact_right(a, b, dims=NN):
    high, low = split2(a)
    rows = a.shape[0]
    both = mul(jnp.concatenate([high, low], axis=0), b, dims)
    return both[:rows] + both[rows:]


def mul3(a, b, dims=NN):
    b_high, b_low = split2(b)
    return mul_exact_right(a, b_high, dims) + mul(a.astype(bf16), b_low, dims)


def iota(shape, dim):
    return lax.broadcasted_iota(jnp.int32, shape, dim)


def kernel(
    n_row, n_col, modes,
    mult_hbm, res_hbm, dir_hbm, eprev_hbm, hyper_hbm, double_hbm, single_hbm, neumann_hbm,
    rigid_hbm, coarse_hbm, face_hbm,
    mult_out, res_out, dir_out,
    mult, res, direc, eprev, hyper, double, single, neumann, rigid, face,
    coarse_all, res_in, dir_in, modes_own, modes_in, one_hot,
    first_own, first_a, first_msg, first_b,
    own2, gather_a2, msg2, gather_b2,
    own3, gather_a3, msg3, gather_b3,
    faces2, faces2_in, faces3, faces3_in,
    local_sem, send_sem, recv_sem,
):
    row = lax.axis_index("row")
    col = lax.axis_index("col")
    cases, width = res.shape[1], res.shape[2]
    nb = double.shape[0]
    lanes = GROUPS * cases

    def at_row(s):
        return (lax.rem(row + s, n_row), col)

    def at_col(s):
        return (row, lax.rem(col + s, n_col))

    neighbours = [at_col(1), at_row(1), at_col(n_col - 1), at_row(n_row - 1)]

    loads = {}
    for i, (name, src, dst) in enumerate([
        ("face", face_hbm, face), ("rigid", rigid_hbm, rigid), ("res", res_hbm, res),
        ("coarse", coarse_hbm, coarse_all.at[0]), ("direc", dir_hbm, direc),
        ("eprev", eprev_hbm, eprev), ("double", double_hbm, double),
        ("hyper", hyper_hbm, hyper), ("single", single_hbm, single),
        ("neumann", neumann_hbm, neumann), ("mult", mult_hbm, mult),
    ]):
        loads[name] = pltpu.make_async_copy(src, dst, local_sem.at[i])
        loads[name].start()

    barrier = pltpu.get_barrier_semaphore()
    for s in range(1, n_row):
        pl.semaphore_signal(barrier, inc=1, device_id=at_row(s), device_id_type=MESH)
    for s in range(1, n_col):
        pl.semaphore_signal(barrier, inc=1, device_id=at_col(s), device_id_type=MESH)
    pl.semaphore_wait(barrier, n_row + n_col - 2)

    sent = []

    def send(src, dst, device):
        i = len(sent)
        copy = pltpu.make_async_remote_copy(
            src_ref=src, dst_ref=dst, send_sem=send_sem.at[i], recv_sem=recv_sem.at[i],
            device_id=device, device_id_type=MESH,
        )
        copy.start()
        sent.append(copy)
        return copy

    res_moves = [send(res_hbm.at[f], res_in.at[f], neighbours[f]) for f in range(2)]
    coarse_moves = [
        send(coarse_hbm, coarse_all.at[1 + (f + 2) % 4], neighbours[f]) for f in range(4)
    ]
    dir_moves = [send(dir_hbm.at[f], dir_in.at[f], neighbours[f]) for f in range(2)]

    loads["face"].wait()
    here = iota((nb, width), 0)
    for f in range(4):
        one_hot[:, f * width:(f + 1) * width] = jnp.where(
            here == face[f:f + 1, :], 1.0, 0.0
        ).astype(bf16)

    loads["rigid"].wait()
    rigid_pad = jnp.concatenate([rigid[...], jnp.zeros((8 - modes, nb), f32)], axis=0)
    modes_face = mul_exact_right(rigid_pad, one_hot[...])
    for f in range(4):
        modes_own[f] = modes_face[:, f * width:(f + 1) * width]
    mode_moves = [
        send(modes_own.at[f], modes_in.at[(f + 2) % 4], neighbours[f]) for f in range(4)
    ]

    lane_at = iota((SLOTS, lanes), 1)
    slot_at = iota((SLOTS, lanes), 0)

    loads["res"].wait()
    for move in res_moves:
        move.wait_recv()
    pieces = jnp.concatenate([res[0], res[1], -res_in[0], -res_in[1]], axis=1)
    g_own = mul3(modes_face, jnp.concatenate([pieces] * GROUPS, axis=0), NT)
    in_group = (lane_at >= slot_at * cases) & (lane_at < (slot_at + 1) * cases)
    first = jnp.sum(jnp.where(in_group, g_own, 0.0), axis=0, keepdims=True)

    def start_rows(message, own, target):
        own[...] = message
        moves = [send(own, target.at[row], at_row(s)) for s in range(1, n_row)]
        target[row] = message
        return moves

    def start_cols(message, own, target):
        own[...] = message
        moves = [send(own, target.at[col], at_col(s)) for s in range(1, n_col)]
        target[col] = message
        return moves

    def finish(moves):
        for move in moves:
            move.wait_recv()

    moves = start_rows(first, first_own, first_a)

    loads["coarse"].wait()
    finish(coarse_moves)
    patches = n_row * n_col
    span = modes * patches
    slot_c = iota((SLOTS, span), 0)
    blocks = []
    for m in range(modes):
        block = jnp.zeros((SLOTS, span), f32)
        for k in range(5):
            block = jnp.where(slot_c == k, coarse_all[k, m:m + 1, :], block)
        blocks.append(block)
    blocks.append(jnp.zeros((lanes - SLOTS * modes, span), f32))
    coarse_rows = jnp.concatenate(blocks, axis=0)
    r_at = iota((n_row, span), 0)
    q_at = iota((n_row, span), 1)
    picks = []
    for j in range(modes):
        for c in range(n_col):
            picks.append(jnp.where(q_at == (r_at * n_col + c) * modes + j, 1.0, 0.0))
    pick = jnp.concatenate(picks, axis=0).astype(bf16)
    coarse_high, coarse_low = split2(coarse_rows)
    solve_high = mul(pick, coarse_high, NT).astype(bf16)
    solve_low = mul(pick, coarse_low, NT).astype(bf16)

    finish(moves)
    moves = start_cols(first_a[:, 0, :], first_msg, first_b)

    finish(mode_moves)
    slot_w = iota((SLOTS, width), 0)
    columns = []
    for f in range(4):
        blocks = []
        for m in range(modes):
            block = jnp.where(slot_w == 0, modes_own[f, m:m + 1, :], 0.0)
            blocks.append(jnp.where(slot_w == 1 + f, -modes_in[f, m:m + 1, :], block))
        columns.append(jnp.concatenate(blocks, axis=0))
    basis = jnp.concatenate(columns, axis=1)
    basis_high, basis_low = split2(basis)
    basis_dof = mul(basis_high, one_hot[...], NT) + mul(basis_low, one_hot[...], NT)
    loads["double"].wait()
    basis_double = 0.5 * basis_dof + mul_exact_right(basis_dof, double[...])

    def correction(g):
        g_t = g.T
        total = jnp.zeros((cases, lanes), f32)
        for j in range(modes):
            rows = slice(j * patches, (j + 1) * patches)
            part = g_t[j * cases:(j + 1) * cases, :]
            total = total + mul_exact_right(part, solve_high[rows])
            total = total + mul(part.astype(bf16), solve_low[rows])
        coef = total[:, :SLOTS * modes]
        return mul_exact_right(coef, basis_high) + mul(coef.astype(bf16), basis_low)

    def message_of(out, scalars):
        message = jnp.zeros((SLOTS, lanes), f32)
        for j in range(modes):
            mask = (lane_at >= j * cases) & (lane_at < (j + 1) * cases)
            message = jnp.where(mask, out[j * SLOTS:(j + 1) * SLOTS], message)
        lane_c = iota((cases, lanes), 1)
        case_c = iota((cases, lanes), 0)
        line = jnp.sum(
            jnp.where(lane_c == case_c + modes * cases, scalars, 0.0), axis=0, keepdims=True
        )
        return message + jnp.where(slot_at == 0, line, 0.0)

    def rolled(x, step):
        step = step % n_row
        return jnp.concatenate([x[n_row - step:], x[:n_row - step]], axis=0)

    def along_rows(buffer):
        own = buffer[:, 0, :] + rolled(buffer[:, 2, :], 1) + rolled(buffer[:, 4, :], -1)
        return jnp.stack([own, buffer[:, 1, :], buffer[:, 3, :]], axis=0)

    def along_cols(buffer):
        tiles = []
        for c in range(n_col):
            tiles.append(
                buffer[c, 0] + buffer[(c - 1) % n_col, 1] + buffer[(c + 1) % n_col, 2]
            )
        return jnp.concatenate(tiles, axis=0)

    def scalars_of(g):
        line = jnp.sum(g, axis=0, keepdims=True)
        lane_c = iota((cases, lanes), 1)
        case_c = iota((cases, lanes), 0)
        return jnp.sum(
            jnp.where(lane_c == case_c + modes * cases, line, 0.0), axis=1, keepdims=True
        )

    def repeated(x):
        return jnp.concatenate([x] * GROUPS, axis=0)

    finish(moves)
    g = jnp.concatenate([first_b[c] for c in range(n_col)], axis=0)
    rounded_faces = (pieces - correction(g)).astype(bf16)
    rounded_full = mul(rounded_faces, one_hot[...], NT)
    rounded = rounded_full.astype(bf16)
    lifted_full = 0.5 * rounded_full + mul(rounded, double[...])
    loads["single"].wait()
    weighed_full = mul(lifted_full.astype(bf16), single[...])
    weighed = weighed_full.astype(bf16)
    weighed_full = weighed.astype(f32)
    loads["hyper"].wait()
    applied = mul(rounded, hyper[...])
    energy_parts = jnp.sum(
        rounded_full * applied + weighed_full * lifted_full, axis=1, keepdims=True
    )
    out = mul3(basis_dof, repeated(applied), NT)
    out = out + mul_exact_right(basis_double, repeated(weighed), NT)
    moves = start_rows(message_of(out, energy_parts), own2, gather_a2)

    applied = applied + 0.5 * weighed_full + mul(weighed, double[...], NT)
    finish(moves)
    moves = start_cols(along_rows(gather_a2), msg2, gather_b2)

    applied_faces = mul_exact_right(applied, one_hot[...])
    for f in range(4):
        faces2[f] = applied_faces[:, f * width:(f + 1) * width]
    face_moves = [
        send(faces2.at[f], faces2_in.at[(f + 2) % 4], neighbours[f]) for f in range(4)
    ]
    loads["direc"].wait()
    finish(dir_moves)
    old_faces = jnp.concatenate([direc[0], direc[1], -dir_in[0], -dir_in[1]], axis=1)
    old_full = mul(old_faces.astype(bf16), one_hot[...], NT)
    loads["neumann"].wait()
    old_applied = mul(old_full.astype(bf16), neumann[...])
    loads["eprev"].wait()
    lane_e = iota((cases, cases), 1)
    case_e = iota((cases, cases), 0)
    energy_prev = jnp.sum(
        jnp.where(lane_e == case_e, eprev[...], 0.0), axis=1, keepdims=True
    )

    finish(face_moves)
    finish(moves)
    g = along_cols(gather_b2)
    energy = scalars_of(g)
    ratio = energy / energy_prev
    jumped = applied_faces - jnp.concatenate([faces2_in[f] for f in range(4)], axis=1)
    searched = jumped - correction(g)
    new_full = mul(searched.astype(bf16), one_hot[...], NT)
    new_applied = mul(new_full.astype(bf16), neumann[...])
    spread_dir = new_full + ratio * old_full
    applied_dir = new_applied + ratio * old_applied
    curvature_parts = jnp.sum(spread_dir * applied_dir, axis=1, keepdims=True)
    out = mul3(basis_dof, repeated(applied_dir), NT)
    moves = start_rows(message_of(out, curvature_parts), own3, gather_a3)
    dir_faces = mul_exact_right(applied_dir, one_hot[...])
    for f in range(2):
        faces3[f] = dir_faces[:, (f + 2) * width:(f + 3) * width]
    face_moves = [send(faces3.at[f], faces3_in.at[f], neighbours[f + 2]) for f in range(2)]
    finish(moves)
    moves = start_cols(along_rows(gather_a3), msg3, gather_b3)
    loads["mult"].wait()
    next_dir = [
        searched[:, f * width:(f + 1) * width] + ratio * direc[f] for f in range(2)
    ]
    for f in range(2):
        dir_out[f] = next_dir[f]
    finish(face_moves)
    finish(moves)
    g = along_cols(gather_b3)
    step = energy / scalars_of(g)
    fix = correction(g)
    for f in range(2):
        part = slice(f * width, (f + 1) * width)
        mult_out[f] = mult[f] + step * next_dir[f]
        res_out[f] = res[f] - step * (dir_faces[:, part] - faces3_in[f] - fix[:, part])

    for copy in sent:
        copy.wait_send()


def on_device(
    multipliers, residual, direction, energy_prev, hypersingular, double_layer,
    single_inverse, neumann_inverse, rigid_modes, coarse_inverse, face_index,
):
    n_row, n_col = lax.axis_size("row"), lax.axis_size("col")
    _, sides, cases, width = residual.shape
    modes, nb = rigid_modes.shape[1:]
    lanes = GROUPS * cases
    values = jax.ShapeDtypeStruct((sides, cases, width), f32)
    matrix = pltpu.VMEM((nb, nb), bf16)
    copies = 12 + 3 * (n_row + n_col - 2) + 6

    def vmem(*shape):
        return pltpu.VMEM(shape, f32)

    outs = pl.pallas_call(
        functools.partial(kernel, n_row, n_col, modes),
        out_shape=(values, values, values),
        in_specs=[pl.BlockSpec(memory_space=pl.ANY)] * 11,
        out_specs=[pl.BlockSpec(memory_space=pltpu.VMEM)] * 3,
        scratch_shapes=[
            vmem(sides, cases, width), vmem(sides, cases, width), vmem(sides, cases, width),
            vmem(1, cases), matrix, matrix, matrix, matrix,
            vmem(modes, nb), pltpu.VMEM(face_index.shape[1:], jnp.int32),
            vmem(5, *coarse_inverse.shape), vmem(2, cases, width), vmem(2, cases, width),
            vmem(4, 8, width), vmem(4, 8, width), pltpu.VMEM((nb, 4 * width), bf16),
            vmem(1, lanes), vmem(n_row, 1, lanes), vmem(n_row, lanes), vmem(n_col, n_row, lanes),
            vmem(SLOTS, lanes), vmem(n_row, SLOTS, lanes),
            vmem(3, n_row, lanes), vmem(n_col, 3, n_row, lanes),
            vmem(SLOTS, lanes), vmem(n_row, SLOTS, lanes),
            vmem(3, n_row, lanes), vmem(n_col, 3, n_row, lanes),
            vmem(4, cases, width), vmem(4, cases, width),
            vmem(2, cases, width), vmem(2, cases, width),
            pltpu.SemaphoreType.DMA((11,)),
            pltpu.SemaphoreType.DMA((copies,)),
            pltpu.SemaphoreType.DMA((copies,)),
        ],
        compiler_params=pltpu.CompilerParams(
            collective_id=0, has_side_effects=True, vmem_limit_bytes=48 * 1024 * 1024
        ),
        cost_estimate=pl.CostEstimate(
            flops=40 * cases * nb * nb, bytes_accessed=8 * nb * nb, transcendentals=0
        ),
    )(
        multipliers[0], residual[0], direction[0], energy_prev.reshape(1, cases),
        hypersingular[0], double_layer[0], single_inverse[0], neumann_inverse[0],
        rigid_modes[0], coarse_inverse, face_index[0],
    )
    return tuple(out[None] for out in outs)


def solution(mesh):
    split = ("row", "col")
    faces = P(split, None, None, None)
    cube = P(split, None, None)
    return jax.shard_map(
        on_device,
        mesh=mesh,
        in_specs=(
            faces, faces, faces, P(), cube, cube, cube, cube, cube, P(split, None), cube,
        ),
        out_specs=(faces, faces, faces),
        check_vma=False,
    )
```

time: 373 us -> 47.7 us (0.13)
  blocking collectives: 233 us -> 0 us
  waiting for transfers between devices: 45.9 us -> 0 us
  local copies, waits for them, and re-layouts: 51.7 us -> 10.4 us
  Pallas kernels: 0 us -> 36.1 us
  starting transfers between devices: 16.2 us -> 0 us
  matrix products: 14.2 us -> 0 us
  other arithmetic: 9.84 us -> 0 us
    all_gather x3 -> x0, blocking collectives: 196 us -> none  [project(): lax.all_gather(partial_value, ('row', 'col'), axis=0, tiled=True)]
    ppermute x20 -> x0, waiting for transfers between devices: 45.9 us -> none  [shifted(): return lax.ppermute(block, axis, route)]
    psum x1 -> x0, blocking collectives: 37.1 us -> none  [on_device(): lax.psum((energy_local, self_local, cross_local, old_local), ('row', 'col'))]
    pallas_call x0 -> x1, Pallas kernels: none -> 36.1 us  [on_device(): pl.pallas_call(functools.partial(kernel, n_row, n_col, modes), out_shape=...]
    gather x7 -> x0, local copies, waits for them, and re-layouts: 22.4 us -> none  [jump_faces(): picked = jnp.take(vectors, face_where, axis=1)]
    scatter x7 -> x0, local copies, waits for them, and re-layouts: 18.4 us -> none  [spread_faces(): jnp.zeros((values.shape[1], NB), jnp.float32).at[:, face_where].set(pieces)]
    ppermute x20 -> x0, starting transfers between devices: 16.2 us -> none  [shifted(): return lax.ppermute(block, axis, route)]
    dot_general x13 -> x0, matrix products: 14.2 us -> none  [the longest x3 4.13 us: project(): lax.dot_general(coarse_coef, rigid_local, contract_first, precision=highest)]
  transfers between devices with their start and end apart: 20 -> 0, of which waited for: 17 -> 0; matrix products, arithmetic and copies ran while one was open for 1% -> 0% of each run, Pallas kernels for 0% -> 0%
where the time goes in v1:
time: 47.7 us; the launch traced here: 47.2 us
  Pallas kernels  36.1 us (76%)
  local copies, waits for them, and re-layouts  10.4 us (22%)
  between operations  0.65 us (1%)
    pallas_call x1, Pallas kernels, on_device(): pl.pallas_call(functools.partial(kernel, n_row, n_col, modes), out_shape=...  36.1 us
    unnamed x20, local copies, waits for them, and re-layouts  10.4 us

profile of v1, /device:TPU:0, one launch (start us, length us, event | category | flops | bytes accessed | tf_op | source)
XLA Modules:
  0.0 47.2 jit_solution(7081561919420826485)
XLA Ops:
  0.6 0.8 %copy.16 = f32[1,6,1152]{2,1,0:T(8,128)S(1)} copy(f32[1,6,1152]{2,0,1:T(1,128)} %param.19) | data formatting | bytes 55296
  1.4 0.0 copy-start
  1.4 1.7 %copy-done = bf16[1,1152,1152]{2,1,0:T(8,128)(2,1)S(1)} copy-done((bf16[1,1152,1152]{2,1,0:T(8,128)(2,1)S(1)}, bf16[1,1152,1152]{2,1,0:T(8,128)(2,1)}, u32[]{:S(2)}) %copy-start) | copy-done | bytes 2654232
  3.1 0.0 copy-start.1
  3.1 1.7 %copy-done.1 = bf16[1,1152,1152]{2,1,0:T(8,128)(2,1)S(1)} copy-done((bf16[1,1152,1152]{2,1,0:T(8,128)(2,1)S(1)}, bf16[1,1152,1152]{2,1,0:T(8,128)(2,1)}, u32[]{:S(2)}) %copy-start.1) | copy-done | bytes 2654232
  4.9 0.0 copy-start.2
  4.9 0.8 %copy-done.2 = f32[1,2,16,256]{3,2,1,0:T(8,128)S(1)} copy-done((f32[1,2,16,256]{3,2,1,0:T(8,128)S(1)}, f32[1,2,16,256]{3,2,1,0:T(8,128)}, u32[]{:S(2)}) %copy-start.2) | copy-done | bytes 32792
  5.6 0.0 copy-start.3
  5.6 0.8 %copy-done.3 = f32[1,2,16,256]{3,2,1,0:T(8,128)S(1)} copy-done((f32[1,2,16,256]{3,2,1,0:T(8,128)S(1)}, f32[1,2,16,256]{3,2,1,0:T(8,128)}, u32[]{:S(2)}) %copy-start.3) | copy-done | bytes 32792
  6.4 0.0 copy-start.4
  6.4 0.8 %copy-done.4 = f32[1,2,16,256]{3,2,1,0:T(8,128)S(1)} copy-done((f32[1,2,16,256]{3,2,1,0:T(8,128)S(1)}, f32[1,2,16,256]{3,2,1,0:T(8,128)}, u32[]{:S(2)}) %copy-start.4) | copy-done | bytes 32792
  7.2 0.0 copy-start.5
  7.2 0.7 %copy-done.5 = f32[6,192]{1,0:T(8,128)S(1)} copy-done((f32[6,192]{1,0:T(8,128)S(1)}, f32[6,192]{1,0:T(8,128)}, u32[]{:S(2)}) %copy-start.5) | copy-done | bytes 4632
  7.9 0.0 copy-start.6
  7.9 0.7 %copy-done.6 = s32[1,4,256]{2,1,0:T(4,128)S(1)} copy-done((s32[1,4,256]{2,1,0:T(4,128)S(1)}, s32[1,4,256]{2,1,0:T(4,128)}, u32[]{:S(2)}) %copy-start.6) | copy-done | bytes 4120
  8.5 0.0 copy-start.7
  8.5 0.7 %copy-done.7 = f32[16]{0:T(128)S(1)} copy-done((f32[16]{0:T(128)S(1)}, f32[16]{0:T(128)}, u32[]{:S(2)}) %copy-start.7) | copy-done | bytes 88
  9.2 36.1 %shard_map.130 = (f32[2,16,256]{2,1,0:T(8,128)S(1)}, f32[2,16,256]{2,1,0:T(8,128)S(1)}, f32[2,16,256]{2,1,0:T(8,128)S(1)}) custom-call(f32[2,16,256]{2,1,0:T(8,128)S(1)} %bitcast.18, f32[2,16,256]{2,1,0:T(8,128)S(1)} %bitcast.19, f32[2,16,256]{2,1,0:T(8,128)S(1)} %bitcast.20, f32[1,16]{1,0:T(1,128)S(1)} %bitcast.25, bf16[1152,1152]{1,0:T(8,128)(2,1)S(1)} %bitcast.15, ...), custom_call_target="tpu_custom_call" | custom-call | flops 849346560 | bytes 10616832 | tf_op jit(solution)/shard_map/pallas_call | solution.py:341
  45.4 0.6 %copy.20 = f32[1,2,16,256]{3,2,1,0:T(8,128)} copy(f32[1,2,16,256]{3,2,1,0:T(8,128)S(1)} %bitcast.23) | data formatting | bytes 65536
  46.0 0.6 %copy.21 = f32[1,2,16,256]{3,2,1,0:T(8,128)} copy(f32[1,2,16,256]{3,2,1,0:T(8,128)S(1)} %bitcast.22) | data formatting | bytes 65536
  46.6 0.6 %copy.22 = f32[1,2,16,256]{3,2,1,0:T(8,128)} copy(f32[1,2,16,256]{3,2,1,0:T(8,128)S(1)} %bitcast.21) | data formatting | bytes 65536
Async XLA Ops:
  1.4 1.7 %copy-start = (bf16[1,1152,1152]{2,1,0:T(8,128)(2,1)S(1)}, bf16[1,1152,1152]{2,1,0:T(8,128)(2,1)}, u32[]{:S(2)}) copy-start(bf16[1,1152,1152]{2,1,0:T(8,128)(2,1)} %param.15) | copy-start | bytes 7962628
  3.1 1.7 %copy-start.1 = (bf16[1,1152,1152]{2,1,0:T(8,128)(2,1)S(1)}, bf16[1,1152,1152]{2,1,0:T(8,128)(2,1)}, u32[]{:S(2)}) copy-start(bf16[1,1152,1152]{2,1,0:T(8,128)(2,1)} %param.16) | copy-start | bytes 7962628
  4.9 0.8 %copy-start.2 = (f32[1,2,16,256]{3,2,1,0:T(8,128)S(1)}, f32[1,2,16,256]{3,2,1,0:T(8,128)}, u32[]{:S(2)}) copy-start(f32[1,2,16,256]{3,2,1,0:T(8,128)} %param.11) | copy-start | bytes 98308
  5.6 0.8 %copy-start.3 = (f32[1,2,16,256]{3,2,1,0:T(8,128)S(1)}, f32[1,2,16,256]{3,2,1,0:T(8,128)}, u32[]{:S(2)}) copy-start(f32[1,2,16,256]{3,2,1,0:T(8,128)} %param.12) | copy-start | bytes 98308
  6.4 0.8 %copy-start.4 = (f32[1,2,16,256]{3,2,1,0:T(8,128)S(1)}, f32[1,2,16,256]{3,2,1,0:T(8,128)}, u32[]{:S(2)}) copy-start(f32[1,2,16,256]{3,2,1,0:T(8,128)} %param.13) | copy-start | bytes 98308
  7.2 0.7 %copy-start.5 = (f32[6,192]{1,0:T(8,128)S(1)}, f32[6,192]{1,0:T(8,128)}, u32[]{:S(2)}) copy-start(f32[6,192]{1,0:T(8,128)} %coarse_hbm.1) | copy-start | bytes 13828
  7.9 0.7 %copy-start.6 = (s32[1,4,256]{2,1,0:T(4,128)S(1)}, s32[1,4,256]{2,1,0:T(4,128)}, u32[]{:S(2)}) copy-start(s32[1,4,256]{2,1,0:T(4,128)} %param.21) | copy-start | bytes 12292
  8.5 0.7 %copy-start.7 = (f32[16]{0:T(128)S(1)}, f32[16]{0:T(128)}, u32[]{:S(2)}) copy-start(f32[16]{0:T(128)} %param.14) | copy-start | bytes 196

commit v2 on v1

--- a/solution.py
+++ b/solution.py
@@ -43,10 +43,10 @@
 
 def kernel(
     n_row, n_col, modes,
-    mult_hbm, res_hbm, dir_hbm, eprev_hbm, hyper_hbm, double_hbm, single_hbm, neumann_hbm,
+    res_hbm, dir_hbm, eprev_hbm, hyper_hbm, double_hbm, single_hbm, neumann_hbm,
     rigid_hbm, coarse_hbm, face_hbm,
-    mult_out, res_out, dir_out,
-    mult, res, direc, eprev, hyper, double, single, neumann, rigid, face,
+    out_ref,
+    res, direc, eprev, hyper, double, single, neumann, rigid, face,
     coarse_all, res_in, dir_in, modes_own, modes_in, one_hot,
     first_own, first_a, first_msg, first_b,
     own2, gather_a2, msg2, gather_b2,
@@ -74,7 +74,7 @@
         ("coarse", coarse_hbm, coarse_all.at[0]), ("direc", dir_hbm, direc),
         ("eprev", eprev_hbm, eprev), ("double", double_hbm, double),
         ("hyper", hyper_hbm, hyper), ("single", single_hbm, single),
-        ("neumann", neumann_hbm, neumann), ("mult", mult_hbm, mult),
+        ("neumann", neumann_hbm, neumann),
     ]):
         loads[name] = pltpu.make_async_copy(src, dst, local_sem.at[i])
         loads[name].start()
@@ -112,7 +112,9 @@
         ).astype(bf16)
 
     loads["rigid"].wait()
-    rigid_pad = jnp.concatenate([rigid[...], jnp.zeros((8 - modes, nb), f32)], axis=0)
+    rigid_pad = jnp.concatenate(
+        [rigid[m] for m in range(modes)] + [jnp.zeros((8 - modes, nb), f32)], axis=0
+    )
     modes_face = mul_exact_right(rigid_pad, one_hot[...])
     for f in range(4):
         modes_own[f] = modes_face[:, f * width:(f + 1) * width]
@@ -187,7 +189,7 @@
         columns.append(jnp.concatenate(blocks, axis=0))
     basis = jnp.concatenate(columns, axis=1)
     basis_high, basis_low = split2(basis)
-    basis_dof = mul(basis_high, one_hot[...], NT) + mul(basis_low, one_hot[...], NT)
+    basis_dof = mul_exact_right(basis, one_hot[...], NT)
     loads["double"].wait()
     basis_double = 0.5 * basis_dof + mul_exact_right(basis_dof, double[...])
 
@@ -273,9 +275,8 @@
     loads["direc"].wait()
     finish(dir_moves)
     old_faces = jnp.concatenate([direc[0], direc[1], -dir_in[0], -dir_in[1]], axis=1)
-    old_full = mul(old_faces.astype(bf16), one_hot[...], NT)
+    old_faces = old_faces.astype(bf16)
     loads["neumann"].wait()
-    old_applied = mul(old_full.astype(bf16), neumann[...])
     loads["eprev"].wait()
     lane_e = iota((cases, cases), 1)
     case_e = iota((cases, cases), 0)
@@ -290,10 +291,11 @@
     ratio = energy / energy_prev
     jumped = applied_faces - jnp.concatenate([faces2_in[f] for f in range(4)], axis=1)
     searched = jumped - correction(g)
-    new_full = mul(searched.astype(bf16), one_hot[...], NT)
-    new_applied = mul(new_full.astype(bf16), neumann[...])
-    spread_dir = new_full + ratio * old_full
-    applied_dir = new_applied + ratio * old_applied
+    paired = jnp.concatenate([searched.astype(bf16), old_faces], axis=0)
+    paired = mul(paired, one_hot[...], NT)
+    paired_applied = mul(paired.astype(bf16), neumann[...])
+    spread_dir = paired[:cases] + ratio * paired[cases:]
+    applied_dir = paired_applied[:cases] + ratio * paired_applied[cases:]
     curvature_parts = jnp.sum(spread_dir * applied_dir, axis=1, keepdims=True)
     out = mul3(basis_dof, repeated(applied_dir), NT)
     moves = start_rows(message_of(out, curvature_parts), own3, gather_a3)
@@ -303,12 +305,12 @@
     face_moves = [send(faces3.at[f], faces3_in.at[f], neighbours[f + 2]) for f in range(2)]
     finish(moves)
     moves = start_cols(along_rows(gather_a3), msg3, gather_b3)
-    loads["mult"].wait()
     next_dir = [
         searched[:, f * width:(f + 1) * width] + ratio * direc[f] for f in range(2)
     ]
     for f in range(2):
-        dir_out[f] = next_dir[f]
+        out_ref[2, f] = searched[:, f * width:(f + 1) * width]
+        out_ref[3, f] = ratio * direc[f]
     finish(face_moves)
     finish(moves)
     g = along_cols(gather_b3)
@@ -316,8 +318,8 @@
     fix = correction(g)
     for f in range(2):
         part = slice(f * width, (f + 1) * width)
-        mult_out[f] = mult[f] + step * next_dir[f]
-        res_out[f] = res[f] - step * (dir_faces[:, part] - faces3_in[f] - fix[:, part])
+        out_ref[0, f] = step * next_dir[f]
+        out_ref[1, f] = step * (dir_faces[:, part] - faces3_in[f] - fix[:, part])
 
     for copy in sent:
         copy.wait_send()
@@ -331,22 +333,21 @@
     _, sides, cases, width = residual.shape
     modes, nb = rigid_modes.shape[1:]
     lanes = GROUPS * cases
-    values = jax.ShapeDtypeStruct((sides, cases, width), f32)
     matrix = pltpu.VMEM((nb, nb), bf16)
     copies = 12 + 3 * (n_row + n_col - 2) + 6
 
     def vmem(*shape):
         return pltpu.VMEM(shape, f32)
 
-    outs = pl.pallas_call(
+    out = pl.pallas_call(
         functools.partial(kernel, n_row, n_col, modes),
-        out_shape=(values, values, values),
-        in_specs=[pl.BlockSpec(memory_space=pl.ANY)] * 11,
-        out_specs=[pl.BlockSpec(memory_space=pltpu.VMEM)] * 3,
+        out_shape=jax.ShapeDtypeStruct((4, sides, cases, width), f32),
+        in_specs=[pl.BlockSpec(memory_space=pltpu.HBM)] * 10,
+        out_specs=pl.BlockSpec(memory_space=pltpu.VMEM),
         scratch_shapes=[
-            vmem(sides, cases, width), vmem(sides, cases, width), vmem(sides, cases, width),
+            vmem(sides, cases, width), vmem(sides, cases, width),
             vmem(1, cases), matrix, matrix, matrix, matrix,
-            vmem(modes, nb), pltpu.VMEM(face_index.shape[1:], jnp.int32),
+            vmem(modes, 1, nb), pltpu.VMEM(face_index.shape[1:], jnp.int32),
             vmem(5, *coarse_inverse.shape), vmem(2, cases, width), vmem(2, cases, width),
             vmem(4, 8, width), vmem(4, 8, width), pltpu.VMEM((nb, 4 * width), bf16),
             vmem(1, lanes), vmem(n_row, 1, lanes), vmem(n_row, lanes), vmem(n_col, n_row, lanes),
@@ -356,22 +357,22 @@
             vmem(3, n_row, lanes), vmem(n_col, 3, n_row, lanes),
             vmem(4, cases, width), vmem(4, cases, width),
             vmem(2, cases, width), vmem(2, cases, width),
-            pltpu.SemaphoreType.DMA((11,)),
+            pltpu.SemaphoreType.DMA((10,)),
             pltpu.SemaphoreType.DMA((copies,)),
             pltpu.SemaphoreType.DMA((copies,)),
         ],
         compiler_params=pltpu.CompilerParams(
-            collective_id=0, has_side_effects=True, vmem_limit_bytes=48 * 1024 * 1024
+            collective_id=0, has_side_effects=True, vmem_limit_bytes=63 * 1024 * 1024
         ),
         cost_estimate=pl.CostEstimate(
             flops=40 * cases * nb * nb, bytes_accessed=8 * nb * nb, transcendentals=0
         ),
     )(
-        multipliers[0], residual[0], direction[0], energy_prev.reshape(1, cases),
+        residual[0], direction[0], energy_prev.reshape(1, cases),
         hypersingular[0], double_layer[0], single_inverse[0], neumann_inverse[0],
-        rigid_modes[0], coarse_inverse, face_index[0],
-    )
-    return tuple(out[None] for out in outs)
+        rigid_modes.transpose(1, 0, 2), coarse_inverse, face_index[0],
+    )
+    return (multipliers + out[0], residual - out[1], (out[2] + out[3])[None])
 
 
 def solution(mesh):

time: 47.7 us -> 38.8 us (0.81)
  local copies, waits for them, and re-layouts: 10.4 us -> 0.01 us
  other arithmetic: 0 us -> 1.45 us
    unnamed x20 -> x4, local copies, waits for them, and re-layouts: 10.4 us -> 0.01 us
    add x0 -> x1, other arithmetic: none -> 1.45 us  [on_device(): return (multipliers + out[0], residual - out[1], (out[2] + out[3])[None])]
where the time goes in v2:
time: 38.8 us; the launch traced here: 38.7 us
  Pallas kernels  36.5 us (94%)
  other arithmetic  1.45 us (4%)
  between operations  0.67 us (2%)
    pallas_call x1, Pallas kernels, on_device(): pl.pallas_call(functools.partial(kernel, n_row, n_col, modes), out_shape=...  36.5 us
    add x1, other arithmetic, on_device(): return (multipliers + out[0], residual - out[1], (out[2] + out[3])[None])  1.45 us

profile of v2, /device:TPU:0, one launch (start us, length us, event | category | flops | bytes accessed | tf_op | source)
XLA Modules:
  0.0 38.7 jit_solution(12247357562713309723)
XLA Ops:
  0.6 0.0 copy-start
  0.6 0.0 copy-start.1
  0.7 36.5 %shard_map.130 = f32[4,2,16,256]{3,2,1,0:T(8,128)} custom-call(f32[2,16,256]{2,1,0:T(8,128)} %bitcast.13, f32[2,16,256]{2,1,0:T(8,128)} %bitcast.14, f32[1,16]{1,0:T(1,128)} %bitcast.17, bf16[1152,1152]{1,0:T(8,128)(2,1)} %bitcast.9, bf16[1152,1152]{1,0:T(8,128)(2,1)} %bitcast.10, bf16[1152,1152]{1,0:T(8,128)(2,1)} %bitcast.11, bf16[1152,1152]{1,0:T(8,128)(2,1)} %bitcast.12, ...), custom_call_target="tpu_custom_call" | custom-call | flops 849346560 | bytes 10616832 | tf_op jit(solution)/shard_map/pallas_call | solution.py:342
  37.2 0.0 copy-done
  37.2 0.0 copy-done.1
  37.2 1.5 %slice_add_fusion = (f32[1,2,16,256]{3,2,1,0:T(8,128)}, f32[1,2,16,256]{3,2,1,0:T(8,128)}, f32[1,2,16,256]{3,2,1,0:T(8,128)}) fusion(f32[4,2,16,256]{3,2,1,0:T(8,128)} %shard_map.130, f32[1,2,16,256]{3,2,1,0:T(8,128)S(1)} %copy-done, f32[1,2,16,256]{3,2,1,0:T(8,128)S(1)} %copy-done.1), kind=kLoop, calls=%fused_computation | loop fusion | flops 24576 | bytes 294912 | tf_op jit(solution)/shard_map/add | solution.py:375
Async XLA Ops:
  0.6 36.6 %copy-start = (f32[1,2,16,256]{3,2,1,0:T(8,128)S(1)}, f32[1,2,16,256]{3,2,1,0:T(8,128)}, u32[]{:S(2)}) copy-start(f32[1,2,16,256]{3,2,1,0:T(8,128)} %param.12) | copy-start | bytes 98308
  0.6 36.6 %copy-start.1 = (f32[1,2,16,256]{3,2,1,0:T(8,128)S(1)}, f32[1,2,16,256]{3,2,1,0:T(8,128)}, u32[]{:S(2)}) copy-start(f32[1,2,16,256]{3,2,1,0:T(8,128)} %param.11) | copy-start | bytes 98308

commit v3 on v2

--- a/solution.py
+++ b/solution.py
@@ -30,11 +30,6 @@
     rows = a.shape[0]
     both = mul(jnp.concatenate([high, low], axis=0), b, dims)
     return both[:rows] + both[rows:]
-
-
-def mul3(a, b, dims=NN):
-    b_high, b_low = split2(b)
-    return mul_exact_right(a, b_high, dims) + mul(a.astype(bf16), b_low, dims)
 
 
 def iota(shape, dim):
@@ -60,6 +55,9 @@
     nb = double.shape[0]
     lanes = GROUPS * cases
 
+    def repeated(x):
+        return jnp.concatenate([x] * GROUPS, axis=0)
+
     def at_row(s):
         return (lax.rem(row + s, n_row), col)
 
@@ -69,15 +67,17 @@
     neighbours = [at_col(1), at_row(1), at_col(n_col - 1), at_row(n_row - 1)]
 
     loads = {}
-    for i, (name, src, dst) in enumerate([
-        ("face", face_hbm, face), ("rigid", rigid_hbm, rigid), ("res", res_hbm, res),
-        ("coarse", coarse_hbm, coarse_all.at[0]), ("direc", dir_hbm, direc),
-        ("eprev", eprev_hbm, eprev), ("double", double_hbm, double),
-        ("hyper", hyper_hbm, hyper), ("single", single_hbm, single),
-        ("neumann", neumann_hbm, neumann),
-    ]):
-        loads[name] = pltpu.make_async_copy(src, dst, local_sem.at[i])
+
+    def load(name, src, dst):
+        loads[name] = pltpu.make_async_copy(src, dst, local_sem.at[len(loads)])
         loads[name].start()
+
+    load("face", face_hbm, face)
+    load("rigid", rigid_hbm, rigid)
+    load("res", res_hbm, res)
+    load("coarse", coarse_hbm, coarse_all.at[0])
+    load("direc", dir_hbm, direc)
+    load("eprev", eprev_hbm, eprev)
 
     barrier = pltpu.get_barrier_semaphore()
     for s in range(1, n_row):
@@ -103,6 +103,10 @@
         send(coarse_hbm, coarse_all.at[1 + (f + 2) % 4], neighbours[f]) for f in range(4)
     ]
     dir_moves = [send(dir_hbm.at[f], dir_in.at[f], neighbours[f]) for f in range(2)]
+    load("double", double_hbm, double)
+    load("single", single_hbm, single)
+    load("hyper", hyper_hbm, hyper)
+    load("neumann", neumann_hbm, neumann)
 
     loads["face"].wait()
     here = iota((nb, width), 0)
@@ -129,7 +133,9 @@
     for move in res_moves:
         move.wait_recv()
     pieces = jnp.concatenate([res[0], res[1], -res_in[0], -res_in[1]], axis=1)
-    g_own = mul3(modes_face, jnp.concatenate([pieces] * GROUPS, axis=0), NT)
+    high, low = split2(pieces)
+    g_own = mul_exact_right(modes_face, repeated(high), NT)
+    g_own = g_own + mul(modes_face.astype(bf16), repeated(low), NT)
     in_group = (lane_at >= slot_at * cases) & (lane_at < (slot_at + 1) * cases)
     first = jnp.sum(jnp.where(in_group, g_own, 0.0), axis=0, keepdims=True)
 
@@ -175,9 +181,6 @@
     solve_high = mul(pick, coarse_high, NT).astype(bf16)
     solve_low = mul(pick, coarse_low, NT).astype(bf16)
 
-    finish(moves)
-    moves = start_cols(first_a[:, 0, :], first_msg, first_b)
-
     finish(mode_moves)
     slot_w = iota((SLOTS, width), 0)
     columns = []
@@ -189,20 +192,36 @@
         columns.append(jnp.concatenate(blocks, axis=0))
     basis = jnp.concatenate(columns, axis=1)
     basis_high, basis_low = split2(basis)
-    basis_dof = mul_exact_right(basis, one_hot[...], NT)
+    rows = SLOTS * modes
+    basis_both = jnp.concatenate([basis_high, basis_low], axis=0)
+    basis_dof = mul(basis_both, one_hot[...], NT)
+    basis_dof = basis_dof[:rows] + basis_dof[rows:]
+    dof_both = jnp.concatenate(split2(basis_dof), axis=0)
+
+    finish(moves)
+    moves = start_cols(first_a[:, 0, :], first_msg, first_b)
+
     loads["double"].wait()
-    basis_double = 0.5 * basis_dof + mul_exact_right(basis_dof, double[...])
-
-    def correction(g):
+    basis_double = mul(dof_both, double[...])
+    basis_double = 0.5 * basis_dof + basis_double[:rows] + basis_double[rows:]
+    double_both = jnp.concatenate(split2(basis_double), axis=0)
+
+    def contributions(vectors):
+        high, low = split2(vectors)
+        both = mul(dof_both, repeated(high), NT)
+        return both[:rows] + both[rows:] + mul(dof_both[:rows], repeated(low), NT)
+
+    def correction(g, columns=4 * width):
         g_t = g.T
         total = jnp.zeros((cases, lanes), f32)
         for j in range(modes):
-            rows = slice(j * patches, (j + 1) * patches)
+            at = slice(j * patches, (j + 1) * patches)
             part = g_t[j * cases:(j + 1) * cases, :]
-            total = total + mul_exact_right(part, solve_high[rows])
-            total = total + mul(part.astype(bf16), solve_low[rows])
-        coef = total[:, :SLOTS * modes]
-        return mul_exact_right(coef, basis_high) + mul(coef.astype(bf16), basis_low)
+            total = total + mul_exact_right(part, solve_high[at])
+            total = total + mul(part.astype(bf16), solve_low[at])
+        coef = total[:, :rows]
+        fix = mul_exact_right(coef, basis_high[:, :columns])
+        return fix + mul(coef.astype(bf16), basis_low[:, :columns])
 
     def message_of(out, scalars):
         message = jnp.zeros((SLOTS, lanes), f32)
@@ -239,9 +258,6 @@
         return jnp.sum(
             jnp.where(lane_c == case_c + modes * cases, line, 0.0), axis=1, keepdims=True
         )
-
-    def repeated(x):
-        return jnp.concatenate([x] * GROUPS, axis=0)
 
     finish(moves)
     g = jnp.concatenate([first_b[c] for c in range(n_col)], axis=0)
@@ -258,20 +274,20 @@
     energy_parts = jnp.sum(
         rounded_full * applied + weighed_full * lifted_full, axis=1, keepdims=True
     )
-    out = mul3(basis_dof, repeated(applied), NT)
-    out = out + mul_exact_right(basis_double, repeated(weighed), NT)
+    from_weighed = mul(double_both, repeated(weighed), NT)
+    out = contributions(applied) + from_weighed[:rows] + from_weighed[rows:]
     moves = start_rows(message_of(out, energy_parts), own2, gather_a2)
 
     applied = applied + 0.5 * weighed_full + mul(weighed, double[...], NT)
-    finish(moves)
-    moves = start_cols(along_rows(gather_a2), msg2, gather_b2)
-
     applied_faces = mul_exact_right(applied, one_hot[...])
     for f in range(4):
         faces2[f] = applied_faces[:, f * width:(f + 1) * width]
     face_moves = [
         send(faces2.at[f], faces2_in.at[(f + 2) % 4], neighbours[f]) for f in range(4)
     ]
+    finish(moves)
+    moves = start_cols(along_rows(gather_a2), msg2, gather_b2)
+
     loads["direc"].wait()
     finish(dir_moves)
     old_faces = jnp.concatenate([direc[0], direc[1], -dir_in[0], -dir_in[1]], axis=1)
@@ -297,7 +313,7 @@
     spread_dir = paired[:cases] + ratio * paired[cases:]
     applied_dir = paired_applied[:cases] + ratio * paired_applied[cases:]
     curvature_parts = jnp.sum(spread_dir * applied_dir, axis=1, keepdims=True)
-    out = mul3(basis_dof, repeated(applied_dir), NT)
+    out = contributions(applied_dir)
     moves = start_rows(message_of(out, curvature_parts), own3, gather_a3)
     dir_faces = mul_exact_right(applied_dir, one_hot[...])
     for f in range(2):
@@ -315,7 +331,7 @@
     finish(moves)
     g = along_cols(gather_b3)
     step = energy / scalars_of(g)
-    fix = correction(g)
+    fix = correction(g, 2 * width)
     for f in range(2):
         part = slice(f * width, (f + 1) * width)
         out_ref[0, f] = step * next_dir[f]

time: 38.8 us -> 37.8 us (0.974)
  Pallas kernels: 36.5 us -> 35.5 us
    pallas_call x1, Pallas kernels: 36.5 us -> 35.5 us  [on_device(): pl.pallas_call(functools.partial(kernel, n_row, n_col, modes), out_shape=...]
where the time goes in v3:
time: 37.8 us; the launch traced here: 37.6 us
  Pallas kernels  35.5 us (94%)
  other arithmetic  1.45 us (4%)
  between operations  0.67 us (2%)
    pallas_call x1, Pallas kernels, on_device(): pl.pallas_call(functools.partial(kernel, n_row, n_col, modes), out_shape=...  35.5 us
    add x1, other arithmetic, on_device(): return (multipliers + out[0], residual - out[1], (out[2] + out[3])[None])  1.45 us

profile of v3, /device:TPU:0, one launch (start us, length us, event | category | flops | bytes accessed | tf_op | source)
XLA Modules:
  0.0 37.6 jit_solution(8295806823417125328)
XLA Ops:
  0.6 0.0 copy-start
  0.6 0.0 copy-start.1
  0.7 35.5 %shard_map.130 = f32[4,2,16,256]{3,2,1,0:T(8,128)} custom-call(f32[2,16,256]{2,1,0:T(8,128)} %bitcast.13, f32[2,16,256]{2,1,0:T(8,128)} %bitcast.14, f32[1,16]{1,0:T(1,128)} %bitcast.17, bf16[1152,1152]{1,0:T(8,128)(2,1)} %bitcast.9, bf16[1152,1152]{1,0:T(8,128)(2,1)} %bitcast.10, bf16[1152,1152]{1,0:T(8,128)(2,1)} %bitcast.11, bf16[1152,1152]{1,0:T(8,128)(2,1)} %bitcast.12, ...), custom_call_target="tpu_custom_call" | custom-call | flops 849346560 | bytes 10616832 | tf_op jit(solution)/shard_map/pallas_call | solution.py:358
  36.1 0.0 copy-done
  36.1 0.0 copy-done.1
  36.1 1.5 %slice_add_fusion = (f32[1,2,16,256]{3,2,1,0:T(8,128)}, f32[1,2,16,256]{3,2,1,0:T(8,128)}, f32[1,2,16,256]{3,2,1,0:T(8,128)}) fusion(f32[4,2,16,256]{3,2,1,0:T(8,128)} %shard_map.130, f32[1,2,16,256]{3,2,1,0:T(8,128)S(1)} %copy-done, f32[1,2,16,256]{3,2,1,0:T(8,128)S(1)} %copy-done.1), kind=kLoop, calls=%fused_computation | loop fusion | flops 24576 | bytes 294912 | tf_op jit(solution)/shard_map/add | solution.py:391
Async XLA Ops:
  0.6 35.5 %copy-start = (f32[1,2,16,256]{3,2,1,0:T(8,128)S(1)}, f32[1,2,16,256]{3,2,1,0:T(8,128)}, u32[]{:S(2)}) copy-start(f32[1,2,16,256]{3,2,1,0:T(8,128)} %param.12) | copy-start | bytes 98308
  0.6 35.5 %copy-start.1 = (f32[1,2,16,256]{3,2,1,0:T(8,128)S(1)}, f32[1,2,16,256]{3,2,1,0:T(8,128)}, u32[]{:S(2)}) copy-start(f32[1,2,16,256]{3,2,1,0:T(8,128)} %param.11) | copy-start | bytes 98308

commit v4 on v3

--- a/solution.py
+++ b/solution.py
@@ -43,11 +43,9 @@
     out_ref,
     res, direc, eprev, hyper, double, single, neumann, rigid, face,
     coarse_all, res_in, dir_in, modes_own, modes_in, one_hot,
-    first_own, first_a, first_msg, first_b,
-    own2, gather_a2, msg2, gather_b2,
-    own3, gather_a3, msg3, gather_b3,
+    own1, gathered1, own2, gathered2, own3, gathered3,
     faces2, faces2_in, faces3, faces3_in,
-    local_sem, send_sem, recv_sem,
+    local_sem, send_sem, recv_sem, gather_send_sem, gather_recv_sem,
 ):
     row = lax.axis_index("row")
     col = lax.axis_index("col")
@@ -79,12 +77,27 @@
     load("direc", dir_hbm, direc)
     load("eprev", eprev_hbm, eprev)
 
+    patches = n_row * n_col
+    me = row * n_col + col
+
+    def other(s):
+        target = lax.rem(me + s, patches)
+        return (lax.div(target, n_col), lax.rem(target, n_col))
+
+    def each_other(body):
+        def step(s, carry):
+            body(s)
+            return carry
+
+        lax.fori_loop(1, patches, step, 0)
+
     barrier = pltpu.get_barrier_semaphore()
-    for s in range(1, n_row):
-        pl.semaphore_signal(barrier, inc=1, device_id=at_row(s), device_id_type=MESH)
-    for s in range(1, n_col):
-        pl.semaphore_signal(barrier, inc=1, device_id=at_col(s), device_id_type=MESH)
-    pl.semaphore_wait(barrier, n_row + n_col - 2)
+    each_other(
+        lambda s: pl.semaphore_signal(
+            barrier, inc=1, device_id=other(s), device_id_type=MESH
+        )
+    )
+    pl.semaphore_wait(barrier, patches - 1)
 
     sent = []
 
@@ -139,27 +152,35 @@
     in_group = (lane_at >= slot_at * cases) & (lane_at < (slot_at + 1) * cases)
     first = jnp.sum(jnp.where(in_group, g_own, 0.0), axis=0, keepdims=True)
 
-    def start_rows(message, own, target):
+    def gather_start(message, own, gathered, parity):
+        slots = gathered.shape[0]
         own[...] = message
-        moves = [send(own, target.at[row], at_row(s)) for s in range(1, n_row)]
-        target[row] = message
-        return moves
-
-    def start_cols(message, own, target):
-        own[...] = message
-        moves = [send(own, target.at[col], at_col(s)) for s in range(1, n_col)]
-        target[col] = message
-        return moves
+        for k in range(slots):
+            gathered[k, col, pl.ds(row, 1), :] = message[k:k + 1, :]
+
+        def copy_of(s):
+            return pltpu.make_async_remote_copy(
+                src_ref=own.at[pl.ds(0, slots)],
+                dst_ref=gathered.at[:, col, row, :],
+                send_sem=gather_send_sem.at[s - 1],
+                recv_sem=gather_recv_sem.at[parity, s - 1],
+                device_id=other(s), device_id_type=MESH,
+            )
+
+        each_other(lambda s: copy_of(s).start())
+        return copy_of
+
+    def gather_finish(copy_of):
+        each_other(lambda s: copy_of(s).wait())
 
     def finish(moves):
         for move in moves:
             move.wait_recv()
 
-    moves = start_rows(first, first_own, first_a)
+    moves = gather_start(first, own1, gathered1, 0)
 
     loads["coarse"].wait()
     finish(coarse_moves)
-    patches = n_row * n_col
     span = modes * patches
     slot_c = iota((SLOTS, span), 0)
     blocks = []
@@ -198,9 +219,6 @@
     basis_dof = basis_dof[:rows] + basis_dof[rows:]
     dof_both = jnp.concatenate(split2(basis_dof), axis=0)
 
-    finish(moves)
-    moves = start_cols(first_a[:, 0, :], first_msg, first_b)
-
     loads["double"].wait()
     basis_double = mul(dof_both, double[...])
     basis_double = 0.5 * basis_dof + basis_double[:rows] + basis_double[rows:]
@@ -239,16 +257,12 @@
         step = step % n_row
         return jnp.concatenate([x[n_row - step:], x[:n_row - step]], axis=0)
 
-    def along_rows(buffer):
-        own = buffer[:, 0, :] + rolled(buffer[:, 2, :], 1) + rolled(buffer[:, 4, :], -1)
-        return jnp.stack([own, buffer[:, 1, :], buffer[:, 3, :]], axis=0)
-
-    def along_cols(buffer):
+    def summed(gathered):
         tiles = []
         for c in range(n_col):
-            tiles.append(
-                buffer[c, 0] + buffer[(c - 1) % n_col, 1] + buffer[(c + 1) % n_col, 2]
-            )
+            total = gathered[0, c] + rolled(gathered[2, c], 1) + rolled(gathered[4, c], -1)
+            total = total + gathered[1, (c - 1) % n_col] + gathered[3, (c + 1) % n_col]
+            tiles.append(total)
         return jnp.concatenate(tiles, axis=0)
 
     def scalars_of(g):
@@ -259,8 +273,8 @@
             jnp.where(lane_c == case_c + modes * cases, line, 0.0), axis=1, keepdims=True
         )
 
-    finish(moves)
-    g = jnp.concatenate([first_b[c] for c in range(n_col)], axis=0)
+    gather_finish(moves)
+    g = jnp.concatenate([gathered1[0, c] for c in range(n_col)], axis=0)
     rounded_faces = (pieces - correction(g)).astype(bf16)
     rounded_full = mul(rounded_faces, one_hot[...], NT)
     rounded = rounded_full.astype(bf16)
@@ -276,7 +290,7 @@
     )
     from_weighed = mul(double_both, repeated(weighed), NT)
     out = contributions(applied) + from_weighed[:rows] + from_weighed[rows:]
-    moves = start_rows(message_of(out, energy_parts), own2, gather_a2)
+    moves = gather_start(message_of(out, energy_parts), own2, gathered2, 1)
 
     applied = applied + 0.5 * weighed_full + mul(weighed, double[...], NT)
     applied_faces = mul_exact_right(applied, one_hot[...])
@@ -285,9 +299,6 @@
     face_moves = [
         send(faces2.at[f], faces2_in.at[(f + 2) % 4], neighbours[f]) for f in range(4)
     ]
-    finish(moves)
-    moves = start_cols(along_rows(gather_a2), msg2, gather_b2)
-
     loads["direc"].wait()
     finish(dir_moves)
     old_faces = jnp.concatenate([direc[0], direc[1], -dir_in[0], -dir_in[1]], axis=1)
@@ -300,13 +311,14 @@
         jnp.where(lane_e == case_e, eprev[...], 0.0), axis=1, keepdims=True
     )
 
-    finish(face_moves)
-    finish(moves)
-    g = along_cols(gather_b2)
+    gather_finish(moves)
+    g = summed(gathered2)
     energy = scalars_of(g)
     ratio = energy / energy_prev
+    fix = correction(g)
+    finish(face_moves)
     jumped = applied_faces - jnp.concatenate([faces2_in[f] for f in range(4)], axis=1)
-    searched = jumped - correction(g)
+    searched = jumped - fix
     paired = jnp.concatenate([searched.astype(bf16), old_faces], axis=0)
     paired = mul(paired, one_hot[...], NT)
     paired_applied = mul(paired.astype(bf16), neumann[...])
@@ -314,24 +326,22 @@
     applied_dir = paired_applied[:cases] + ratio * paired_applied[cases:]
     curvature_parts = jnp.sum(spread_dir * applied_dir, axis=1, keepdims=True)
     out = contributions(applied_dir)
-    moves = start_rows(message_of(out, curvature_parts), own3, gather_a3)
+    moves = gather_start(message_of(out, curvature_parts), own3, gathered3, 0)
     dir_faces = mul_exact_right(applied_dir, one_hot[...])
     for f in range(2):
         faces3[f] = dir_faces[:, (f + 2) * width:(f + 3) * width]
     face_moves = [send(faces3.at[f], faces3_in.at[f], neighbours[f + 2]) for f in range(2)]
-    finish(moves)
-    moves = start_cols(along_rows(gather_a3), msg3, gather_b3)
     next_dir = [
         searched[:, f * width:(f + 1) * width] + ratio * direc[f] for f in range(2)
     ]
     for f in range(2):
         out_ref[2, f] = searched[:, f * width:(f + 1) * width]
         out_ref[3, f] = ratio * direc[f]
-    finish(face_moves)
-    finish(moves)
-    g = along_cols(gather_b3)
+    gather_finish(moves)
+    g = summed(gathered3)
     step = energy / scalars_of(g)
     fix = correction(g, 2 * width)
+    finish(face_moves)
     for f in range(2):
         part = slice(f * width, (f + 1) * width)
         out_ref[0, f] = step * next_dir[f]
@@ -350,7 +360,7 @@
     modes, nb = rigid_modes.shape[1:]
     lanes = GROUPS * cases
     matrix = pltpu.VMEM((nb, nb), bf16)
-    copies = 12 + 3 * (n_row + n_col - 2) + 6
+    copies = 18
 
     def vmem(*shape):
         return pltpu.VMEM(shape, f32)
@@ -366,16 +376,16 @@
             vmem(modes, 1, nb), pltpu.VMEM(face_index.shape[1:], jnp.int32),
             vmem(5, *coarse_inverse.shape), vmem(2, cases, width), vmem(2, cases, width),
             vmem(4, 8, width), vmem(4, 8, width), pltpu.VMEM((nb, 4 * width), bf16),
-            vmem(1, lanes), vmem(n_row, 1, lanes), vmem(n_row, lanes), vmem(n_col, n_row, lanes),
-            vmem(SLOTS, lanes), vmem(n_row, SLOTS, lanes),
-            vmem(3, n_row, lanes), vmem(n_col, 3, n_row, lanes),
-            vmem(SLOTS, lanes), vmem(n_row, SLOTS, lanes),
-            vmem(3, n_row, lanes), vmem(n_col, 3, n_row, lanes),
+            vmem(1, lanes), vmem(1, n_col, n_row, lanes),
+            vmem(SLOTS, lanes), vmem(5, n_col, n_row, lanes),
+            vmem(SLOTS, lanes), vmem(5, n_col, n_row, lanes),
             vmem(4, cases, width), vmem(4, cases, width),
             vmem(2, cases, width), vmem(2, cases, width),
             pltpu.SemaphoreType.DMA((10,)),
             pltpu.SemaphoreType.DMA((copies,)),
             pltpu.SemaphoreType.DMA((copies,)),
+            pltpu.SemaphoreType.DMA((n_row * n_col - 1,)),
+            pltpu.SemaphoreType.DMA((2, n_row * n_col - 1)),
         ],
         compiler_params=pltpu.CompilerParams(
             collective_id=0, has_side_effects=True, vmem_limit_bytes=63 * 1024 * 1024

time: 37.8 us -> 33.3 us (0.88)
  Pallas kernels: 35.5 us -> 31 us
    pallas_call x1, Pallas kernels: 35.5 us -> 31 us  [on_device(): pl.pallas_call(functools.partial(kernel, n_row, n_col, modes), out_shape=...]
where the time goes in v4:
time: 33.3 us; the launch traced here: 33.1 us
  Pallas kernels  31 us (93%)
  other arithmetic  1.45 us (4%)
  between operations  0.67 us (2%)
    pallas_call x1, Pallas kernels, on_device(): pl.pallas_call(functools.partial(kernel, n_row, n_col, modes), out_shape=...  31 us
    add x1, other arithmetic, on_device(): return (multipliers + out[0], residual - out[1], (out[2] + out[3])[None])  1.45 us

profile of v4, /device:TPU:0, one launch (start us, length us, event | category | flops | bytes accessed | tf_op | source)
XLA Modules:
  0.0 33.1 jit_solution(18335359336917223850)
XLA Ops:
  0.6 0.0 copy-start
  0.6 0.0 copy-start.1
  0.7 31.0 %shard_map.130 = f32[4,2,16,256]{3,2,1,0:T(8,128)} custom-call(f32[2,16,256]{2,1,0:T(8,128)} %bitcast.13, f32[2,16,256]{2,1,0:T(8,128)} %bitcast.14, f32[1,16]{1,0:T(1,128)} %bitcast.17, bf16[1152,1152]{1,0:T(8,128)(2,1)} %bitcast.9, bf16[1152,1152]{1,0:T(8,128)(2,1)} %bitcast.10, bf16[1152,1152]{1,0:T(8,128)(2,1)} %bitcast.11, bf16[1152,1152]{1,0:T(8,128)(2,1)} %bitcast.12, ...), custom_call_target="tpu_custom_call" | custom-call | flops 849346560 | bytes 10616832 | tf_op jit(solution)/shard_map/pallas_call | solution.py:368
  31.6 0.0 copy-done
  31.7 0.0 copy-done.1
  31.7 1.5 %slice_add_fusion = (f32[1,2,16,256]{3,2,1,0:T(8,128)}, f32[1,2,16,256]{3,2,1,0:T(8,128)}, f32[1,2,16,256]{3,2,1,0:T(8,128)}) fusion(f32[4,2,16,256]{3,2,1,0:T(8,128)} %shard_map.130, f32[1,2,16,256]{3,2,1,0:T(8,128)S(1)} %copy-done, f32[1,2,16,256]{3,2,1,0:T(8,128)S(1)} %copy-done.1), kind=kLoop, calls=%fused_computation | loop fusion | flops 24576 | bytes 294912 | tf_op jit(solution)/shard_map/add | solution.py:401
Async XLA Ops:
  0.6 31.0 %copy-start = (f32[1,2,16,256]{3,2,1,0:T(8,128)S(1)}, f32[1,2,16,256]{3,2,1,0:T(8,128)}, u32[]{:S(2)}) copy-start(f32[1,2,16,256]{3,2,1,0:T(8,128)} %param.12) | copy-start | bytes 98308
  0.6 31.0 %copy-start.1 = (f32[1,2,16,256]{3,2,1,0:T(8,128)S(1)}, f32[1,2,16,256]{3,2,1,0:T(8,128)}, u32[]{:S(2)}) copy-start(f32[1,2,16,256]{3,2,1,0:T(8,128)} %param.11) | copy-start | bytes 98308

commit v5 on v4

--- a/solution.py
+++ b/solution.py
@@ -78,25 +78,32 @@
     load("eprev", eprev_hbm, eprev)
 
     patches = n_row * n_col
-    me = row * n_col + col
-
-    def other(s):
-        target = lax.rem(me + s, patches)
-        return (lax.div(target, n_col), lax.rem(target, n_col))
 
     def each_other(body):
-        def step(s, carry):
-            body(s)
+        for j in range(1, n_col):
+            body(j, (row, lax.rem(col + j, n_col)))
+
+        def step(i, carry):
+            there = lax.rem(row + i, n_row)
+            for j in range(n_col):
+                body(i * n_col + j, (there, lax.rem(col + j, n_col)))
             return carry
 
-        lax.fori_loop(1, patches, step, 0)
+        lax.fori_loop(1, n_row, step, 0)
 
     barrier = pltpu.get_barrier_semaphore()
     each_other(
-        lambda s: pl.semaphore_signal(
-            barrier, inc=1, device_id=other(s), device_id_type=MESH
+        lambda s, device: pl.semaphore_signal(
+            barrier, inc=1, device_id=device, device_id_type=MESH
         )
     )
+
+    loads["face"].wait()
+    here = iota((nb, width), 0)
+    for f in range(4):
+        one_hot[:, f * width:(f + 1) * width] = jnp.where(
+            here == face[f:f + 1, :], 1.0, 0.0
+        ).astype(bf16)
     pl.semaphore_wait(barrier, patches - 1)
 
     sent = []
@@ -121,13 +128,6 @@
     load("hyper", hyper_hbm, hyper)
     load("neumann", neumann_hbm, neumann)
 
-    loads["face"].wait()
-    here = iota((nb, width), 0)
-    for f in range(4):
-        one_hot[:, f * width:(f + 1) * width] = jnp.where(
-            here == face[f:f + 1, :], 1.0, 0.0
-        ).astype(bf16)
-
     loads["rigid"].wait()
     rigid_pad = jnp.concatenate(
         [rigid[m] for m in range(modes)] + [jnp.zeros((8 - modes, nb), f32)], axis=0
@@ -158,26 +158,29 @@
         for k in range(slots):
             gathered[k, col, pl.ds(row, 1), :] = message[k:k + 1, :]
 
-        def copy_of(s):
+        def copy_of(s, device):
             return pltpu.make_async_remote_copy(
                 src_ref=own.at[pl.ds(0, slots)],
                 dst_ref=gathered.at[:, col, row, :],
-                send_sem=gather_send_sem.at[s - 1],
+                send_sem=gather_send_sem.at[parity, s - 1],
                 recv_sem=gather_recv_sem.at[parity, s - 1],
-                device_id=other(s), device_id_type=MESH,
+                device_id=device, device_id_type=MESH,
             )
 
-        each_other(lambda s: copy_of(s).start())
+        each_other(lambda s, device: copy_of(s, device).start())
         return copy_of
 
     def gather_finish(copy_of):
-        each_other(lambda s: copy_of(s).wait())
+        each_other(lambda s, device: copy_of(s, device).wait_recv())
+
+    def gather_sent(copy_of):
+        each_other(lambda s, device: copy_of(s, device).wait_send())
 
     def finish(moves):
         for move in moves:
             move.wait_recv()
 
-    moves = gather_start(first, own1, gathered1, 0)
+    gather1 = gather_start(first, own1, gathered1, 0)
 
     loads["coarse"].wait()
     finish(coarse_moves)
@@ -273,7 +276,7 @@
             jnp.where(lane_c == case_c + modes * cases, line, 0.0), axis=1, keepdims=True
         )
 
-    gather_finish(moves)
+    gather_finish(gather1)
     g = jnp.concatenate([gathered1[0, c] for c in range(n_col)], axis=0)
     rounded_faces = (pieces - correction(g)).astype(bf16)
     rounded_full = mul(rounded_faces, one_hot[...], NT)
@@ -290,7 +293,7 @@
     )
     from_weighed = mul(double_both, repeated(weighed), NT)
     out = contributions(applied) + from_weighed[:rows] + from_weighed[rows:]
-    moves = gather_start(message_of(out, energy_parts), own2, gathered2, 1)
+    gather2 = gather_start(message_of(out, energy_parts), own2, gathered2, 1)
 
     applied = applied + 0.5 * weighed_full + mul(weighed, double[...], NT)
     applied_faces = mul_exact_right(applied, one_hot[...])
@@ -311,7 +314,8 @@
         jnp.where(lane_e == case_e, eprev[...], 0.0), axis=1, keepdims=True
     )
 
-    gather_finish(moves)
+    gather_sent(gather1)
+    gather_finish(gather2)
     g = summed(gathered2)
     energy = scalars_of(g)
     ratio = energy / energy_prev
@@ -326,7 +330,7 @@
     applied_dir = paired_applied[:cases] + ratio * paired_applied[cases:]
     curvature_parts = jnp.sum(spread_dir * applied_dir, axis=1, keepdims=True)
     out = contributions(applied_dir)
-    moves = gather_start(message_of(out, curvature_parts), own3, gathered3, 0)
+    gather3 = gather_start(message_of(out, curvature_parts), own3, gathered3, 0)
     dir_faces = mul_exact_right(applied_dir, one_hot[...])
     for f in range(2):
         faces3[f] = dir_faces[:, (f + 2) * width:(f + 3) * width]
@@ -337,7 +341,8 @@
     for f in range(2):
         out_ref[2, f] = searched[:, f * width:(f + 1) * width]
         out_ref[3, f] = ratio * direc[f]
-    gather_finish(moves)
+    gather_sent(gather2)
+    gather_finish(gather3)
     g = summed(gathered3)
     step = energy / scalars_of(g)
     fix = correction(g, 2 * width)
@@ -347,6 +352,7 @@
         out_ref[0, f] = step * next_dir[f]
         out_ref[1, f] = step * (dir_faces[:, part] - faces3_in[f] - fix[:, part])
 
+    gather_sent(gather3)
     for copy in sent:
         copy.wait_send()
 
@@ -384,7 +390,7 @@
             pltpu.SemaphoreType.DMA((10,)),
             pltpu.SemaphoreType.DMA((copies,)),
             pltpu.SemaphoreType.DMA((copies,)),
-            pltpu.SemaphoreType.DMA((n_row * n_col - 1,)),
+            pltpu.SemaphoreType.DMA((2, n_row * n_col - 1)),
             pltpu.SemaphoreType.DMA((2, n_row * n_col - 1)),
         ],
         compiler_params=pltpu.CompilerParams(

time: 33.3 us -> 33.4 us (level)
  no operation moved by 1% of the time
where the time goes in v5:
time: 33.4 us; the launch traced here: 33.1 us
  Pallas kernels  31 us (93%)
  other arithmetic  1.45 us (4%)
  between operations  0.67 us (2%)
    pallas_call x1, Pallas kernels, on_device(): pl.pallas_call(functools.partial(kernel, n_row, n_col, modes), out_shape=...  31 us
    add x1, other arithmetic, on_device(): return (multipliers + out[0], residual - out[1], (out[2] + out[3])[None])  1.45 us

profile of v5, /device:TPU:0, one launch (start us, length us, event | category | flops | bytes accessed | tf_op | source)
XLA Modules:
  0.0 33.1 jit_solution(12636424408827128757)
XLA Ops:
  0.6 0.0 copy-start
  0.6 0.0 copy-start.1
  0.7 31.0 %shard_map.130 = f32[4,2,16,256]{3,2,1,0:T(8,128)} custom-call(f32[2,16,256]{2,1,0:T(8,128)} %bitcast.13, f32[2,16,256]{2,1,0:T(8,128)} %bitcast.14, f32[1,16]{1,0:T(1,128)} %bitcast.17, bf16[1152,1152]{1,0:T(8,128)(2,1)} %bitcast.9, bf16[1152,1152]{1,0:T(8,128)(2,1)} %bitcast.10, bf16[1152,1152]{1,0:T(8,128)(2,1)} %bitcast.11, bf16[1152,1152]{1,0:T(8,128)(2,1)} %bitcast.12, ...), custom_call_target="tpu_custom_call" | custom-call | flops 849346560 | bytes 10616832 | tf_op jit(solution)/shard_map/pallas_call | solution.py:374
  31.7 0.0 copy-done
  31.7 0.0 copy-done.1
  31.7 1.5 %slice_add_fusion = (f32[1,2,16,256]{3,2,1,0:T(8,128)}, f32[1,2,16,256]{3,2,1,0:T(8,128)}, f32[1,2,16,256]{3,2,1,0:T(8,128)}) fusion(f32[4,2,16,256]{3,2,1,0:T(8,128)} %shard_map.130, f32[1,2,16,256]{3,2,1,0:T(8,128)S(1)} %copy-done, f32[1,2,16,256]{3,2,1,0:T(8,128)S(1)} %copy-done.1), kind=kLoop, calls=%fused_computation | loop fusion | flops 24576 | bytes 294912 | tf_op jit(solution)/shard_map/add | solution.py:407
Async XLA Ops:
  0.6 31.0 %copy-start = (f32[1,2,16,256]{3,2,1,0:T(8,128)S(1)}, f32[1,2,16,256]{3,2,1,0:T(8,128)}, u32[]{:S(2)}) copy-start(f32[1,2,16,256]{3,2,1,0:T(8,128)} %param.12) | copy-start | bytes 98308
  0.6 31.0 %copy-start.1 = (f32[1,2,16,256]{3,2,1,0:T(8,128)S(1)}, f32[1,2,16,256]{3,2,1,0:T(8,128)}, u32[]{:S(2)}) copy-start(f32[1,2,16,256]{3,2,1,0:T(8,128)} %param.11) | copy-start | bytes 98308

commit v6 on v4

--- a/solution.py
+++ b/solution.py
@@ -42,7 +42,7 @@
     rigid_hbm, coarse_hbm, face_hbm,
     out_ref,
     res, direc, eprev, hyper, double, single, neumann, rigid, face,
-    coarse_all, res_in, dir_in, modes_own, modes_in, one_hot,
+    coarse_all, res_in, dir_in, modes_own, modes_in, one_hot, one_hot_t,
     own1, gathered1, own2, gathered2, own3, gathered3,
     faces2, faces2_in, faces3, faces3_in,
     local_sem, send_sem, recv_sem, gather_send_sem, gather_recv_sem,
@@ -178,6 +178,14 @@
             move.wait_recv()
 
     moves = gather_start(first, own1, gathered1, 0)
+
+    face_rows = face[...].astype(f32)
+    face_columns = jnp.concatenate([face_rows, jnp.zeros((4, width), f32)], axis=0).T
+    there = iota((width, nb), 1).astype(f32)
+    for f in range(4):
+        one_hot_t[f * width:(f + 1) * width, :] = jnp.where(
+            there == face_columns[:, f:f + 1], 1.0, 0.0
+        ).astype(bf16)
 
     loads["coarse"].wait()
     finish(coarse_moves)
@@ -215,7 +223,7 @@
     basis_high, basis_low = split2(basis)
     rows = SLOTS * modes
     basis_both = jnp.concatenate([basis_high, basis_low], axis=0)
-    basis_dof = mul(basis_both, one_hot[...], NT)
+    basis_dof = mul(basis_both, one_hot_t[...])
     basis_dof = basis_dof[:rows] + basis_dof[rows:]
     dof_both = jnp.concatenate(split2(basis_dof), axis=0)
 
@@ -276,7 +284,7 @@
     gather_finish(moves)
     g = jnp.concatenate([gathered1[0, c] for c in range(n_col)], axis=0)
     rounded_faces = (pieces - correction(g)).astype(bf16)
-    rounded_full = mul(rounded_faces, one_hot[...], NT)
+    rounded_full = mul(rounded_faces, one_hot_t[...])
     rounded = rounded_full.astype(bf16)
     lifted_full = 0.5 * rounded_full + mul(rounded, double[...])
     loads["single"].wait()
@@ -320,7 +328,7 @@
     jumped = applied_faces - jnp.concatenate([faces2_in[f] for f in range(4)], axis=1)
     searched = jumped - fix
     paired = jnp.concatenate([searched.astype(bf16), old_faces], axis=0)
-    paired = mul(paired, one_hot[...], NT)
+    paired = mul(paired, one_hot_t[...])
     paired_applied = mul(paired.astype(bf16), neumann[...])
     spread_dir = paired[:cases] + ratio * paired[cases:]
     applied_dir = paired_applied[:cases] + ratio * paired_applied[cases:]
@@ -376,6 +384,7 @@
             vmem(modes, 1, nb), pltpu.VMEM(face_index.shape[1:], jnp.int32),
             vmem(5, *coarse_inverse.shape), vmem(2, cases, width), vmem(2, cases, width),
             vmem(4, 8, width), vmem(4, 8, width), pltpu.VMEM((nb, 4 * width), bf16),
+            pltpu.VMEM((4 * width, nb), bf16),
             vmem(1, lanes), vmem(1, n_col, n_row, lanes),
             vmem(SLOTS, lanes), vmem(5, n_col, n_row, lanes),
             vmem(SLOTS, lanes), vmem(5, n_col, n_row, lanes),

time: 33.3 us -> 32.7 us (0.982)
  Pallas kernels: 31 us -> 30.4 us
    pallas_call x1, Pallas kernels: 31 us -> 30.4 us  [on_device(): pl.pallas_call(functools.partial(kernel, n_row, n_col, modes), out_shape=...]
where the time goes in v6:
time: 32.7 us; the launch traced here: 32.5 us
  Pallas kernels  30.4 us (93%)
  other arithmetic  1.45 us (4%)
  between operations  0.67 us (2%)
    pallas_call x1, Pallas kernels, on_device(): pl.pallas_call(functools.partial(kernel, n_row, n_col, modes), out_shape=...  30.4 us
    add x1, other arithmetic, on_device(): return (multipliers + out[0], residual - out[1], (out[2] + out[3])[None])  1.45 us

profile of v6, /device:TPU:0, one launch (start us, length us, event | category | flops | bytes accessed | tf_op | source)
XLA Modules:
  0.0 32.5 jit_solution(16769865505182412194)
XLA Ops:
  0.6 0.0 copy-start
  0.6 0.0 copy-start.1
  0.7 30.4 %shard_map.130 = f32[4,2,16,256]{3,2,1,0:T(8,128)} custom-call(f32[2,16,256]{2,1,0:T(8,128)} %bitcast.13, f32[2,16,256]{2,1,0:T(8,128)} %bitcast.14, f32[1,16]{1,0:T(1,128)} %bitcast.17, bf16[1152,1152]{1,0:T(8,128)(2,1)} %bitcast.9, bf16[1152,1152]{1,0:T(8,128)(2,1)} %bitcast.10, bf16[1152,1152]{1,0:T(8,128)(2,1)} %bitcast.11, bf16[1152,1152]{1,0:T(8,128)(2,1)} %bitcast.12, ...), custom_call_target="tpu_custom_call" | custom-call | flops 849346560 | bytes 10616832 | tf_op jit(solution)/shard_map/pallas_call | solution.py:376
  31.0 0.0 copy-done
  31.0 0.0 copy-done.1
  31.0 1.5 %slice_add_fusion = (f32[1,2,16,256]{3,2,1,0:T(8,128)}, f32[1,2,16,256]{3,2,1,0:T(8,128)}, f32[1,2,16,256]{3,2,1,0:T(8,128)}) fusion(f32[4,2,16,256]{3,2,1,0:T(8,128)} %shard_map.130, f32[1,2,16,256]{3,2,1,0:T(8,128)S(1)} %copy-done, f32[1,2,16,256]{3,2,1,0:T(8,128)S(1)} %copy-done.1), kind=kLoop, calls=%fused_computation | loop fusion | flops 24576 | bytes 294912 | tf_op jit(solution)/shard_map/add | solution.py:410
Async XLA Ops:
  0.6 30.4 %copy-start = (f32[1,2,16,256]{3,2,1,0:T(8,128)S(1)}, f32[1,2,16,256]{3,2,1,0:T(8,128)}, u32[]{:S(2)}) copy-start(f32[1,2,16,256]{3,2,1,0:T(8,128)} %param.12) | copy-start | bytes 98308
  0.6 30.4 %copy-start.1 = (f32[1,2,16,256]{3,2,1,0:T(8,128)S(1)}, f32[1,2,16,256]{3,2,1,0:T(8,128)}, u32[]{:S(2)}) copy-start(f32[1,2,16,256]{3,2,1,0:T(8,128)} %param.11) | copy-start | bytes 98308
